TPU v7x, 256 devices: a whole 4x4x8 slice. The times are simulated.
256 devices in a mesh: cx: 32 (over y, x, core), tp: 8 (over z).
Axes of the slice: x: 4, y: 4, z: 8, core: 2. Of those that a mesh axis runs over, the one named last changes fastest.
Arguments:
- layer_input: bfloat16 [4096, 3072], P('cx', 'tp'), may hold values from -40 to 40
- queries: bfloat16 [4096, 4096], P('cx', 'tp'), may hold values from -6 to 6
- keys: bfloat16 [4096, 4096], P('cx', 'tp'), may hold values from -6 to 6
- values: bfloat16 [4096, 4096], P('cx', 'tp'), may hold values from -6 to 6
- gate_input: bfloat16 [4096, 4096], P('cx', 'tp'), may hold values from -6 to 6
- log_decay: float32 [32, 4096], P('tp', 'cx'), may hold values from -1 to 0
- prior_state: float32 [32, 128, 128], P('tp'), may hold values from -192 to 192
- attn_gain: float32 [4096], P('tp'), may hold values from 0.5 to 1.5
- out_weight: bfloat16 [4096, 3072], P('tp'), may hold values from -0.09375 to 0.09375
- moe_gain: float32 [3072], replicated, may hold values from 0.5 to 1.5
- router: bfloat16 [3072, 16], replicated, may hold values from -0.109375 to 0.109375
- expert_ids: int32 [4096, 2], P('cx'), may hold values from 0 to 15, all different within a row; in each aligned block of 128 rows (0 to 127, 128 to 255, ...) at most 32 rows name the same one
- w_gate: bfloat16 [32, 3072, 3072], P('cx', None, 'tp'), may hold values from -0.109375 to 0.109375
- w_up: bfloat16 [32, 3072, 3072], P('cx', None, 'tp'), may hold values from -0.109375 to 0.109375
- w_down: bfloat16 [32, 3072, 3072], P('cx', 'tp'), may hold values from -0.078125 to 0.078125
Outputs:
- mixed: bfloat16 [4096, 3072], P('cx', 'tp')
Inputs may be any that keep to these rules, and one draw needn't show every extreme that they name: `expert_ids`: each row names 2 different experts. Among the rows of one index of cx no expert is named by more than 32 rows, and in every draw some expert is named by exactly 32 of them.
All inputs are finite; a program needn't handle non-finite values.
Results may differ from a plain program's by a relative error of at most 0.0085.
Values may be sent and summed in bfloat16 or wider, within the bound.
No kernel may reach another device: no remote copies, remote signals or barrier semaphores. Data moves between devices by JAX's collectives and lax.ppermute only.
A program may use at most 128 MiB of HBM per device.

v0:
```python
import functools

import jax
import jax.numpy as jnp
from jax import lax
from jax.experimental import pallas as pl
from jax.experimental.pallas import tpu as pltpu
from jax.sharding import Mesh, PartitionSpec as P

epsilon = 1e-06
exact = lax.Precision.HIGHEST
bf16 = jnp.bfloat16
f32 = jnp.float32
LIMIT = 30 << 20


def mm(a, b, contract_a=1, contract_b=0, precision=None):
    return lax.dot_general(
        a, b, (((contract_a,), (contract_b,)), ((), ())),
        precision=precision, preferred_element_type=f32,
    )


def lower_triangle(n, strict=False):
    rows = lax.broadcasted_iota(jnp.int32, (n, n), 0)
    cols = lax.broadcasted_iota(jnp.int32, (n, n), 1)
    return (rows > cols) if strict else (rows >= cols)


def block_state_kernel(keys, values, log_decay, ids, out, *, experts, capacity):
    heads, positions = log_decay.shape
    size = keys.shape[1] // heads
    per_head = out.shape[1]
    rows = size // per_head
    until = mm(lower_triangle(positions).astype(f32), log_decay[...], 1, 1, exact)
    first, second = slots_of(ids[...], experts, capacity)
    chosen = [jnp.broadcast_to(ids[k:k + 1, :].astype(f32), (8, positions)).astype(bf16) for k in range(2)]
    others = mm(chosen[1], first.astype(bf16), 1, 1) + mm(chosen[0], second.astype(bf16), 1, 1)
    for h in range(heads):
        lanes = slice(h * size, (h + 1) * size)
        total = until[positions - 1:positions, h:h + 1]
        trailing = jnp.exp(total - until[:, h:h + 1])
        weighted = (keys[:, lanes].astype(f32) * trailing).astype(bf16)
        state = mm(weighted, values[:, lanes], 0, 0)
        out[h, :, :rows, :] = state.astype(bf16).reshape(per_head, rows, size)
        high = total.astype(bf16).astype(f32)
        middle = (total - high).astype(bf16).astype(f32)
        low = total - high - middle
        row = lax.broadcasted_iota(jnp.int32, (rows, size), 0)
        terms = jnp.where(row == 0, high, jnp.where(row == 1, middle, jnp.where(row == 2, low, 0.0)))
        terms = jnp.where(row == 3, others[0:1, lanes], terms)
        out[h, :, rows:, :] = jnp.broadcast_to(terms.astype(bf16), (per_head, rows, size))


def load_part_kernel(part, source, target, sem):
    rows = target.shape[0]
    copy = pltpu.make_async_copy(source.at[pl.ds(pl.multiple_of(part[0] * rows, rows), rows)], target, sem)
    copy.start()
    copy.wait()


def state_scan_kernel(received, prior, out, others):
    blocks, rows, _ = out.shape
    state = prior[...]
    for k in range(blocks):
        out[k] = state.astype(bf16)
        terms = received[k, rows:, :].astype(f32)
        total = terms[0:1] + terms[1:2] + terms[2:3]
        state = jnp.exp(total) * state + received[k, :rows, :].astype(f32)
        others[k:k + 1, :] = terms[3:4]


def inner_kernel(queries, keys, values, log_decay, out, growth):
    heads, positions = log_decay.shape
    size = queries.shape[1] // heads
    causal = lower_triangle(positions)
    until = mm(causal.astype(f32), log_decay[...], 1, 1, exact)
    until_row = mm(log_decay[...], causal.astype(f32), 1, 1, exact)
    for h in range(heads):
        lanes = slice(h * size, (h + 1) * size)
        spread = until[:, h:h + 1] - until_row[h:h + 1, :]
        weights = jnp.where(causal, jnp.exp(jnp.where(causal, spread, 0.0)), 0.0)
        scores = mm(queries[:, lanes], keys[:, lanes], 1, 1) * weights
        out[:, lanes] = mm(scores.astype(bf16), values[:, lanes])
    growth[...] = jnp.exp(until)


def project_kernel(queries, inner, growth, state, gate_input, gain, weight, out, *, heads):
    size = queries.shape[1] // heads
    normed = []
    for h in range(heads):
        lanes = slice(h * size, (h + 1) * size)
        carried = mm(queries[:, lanes], state[lanes, :])
        attended = inner[:, lanes] + growth[:, h:h + 1] * carried
        squares = jnp.mean(attended * attended, axis=1, keepdims=True)
        gating = jax.nn.sigmoid(gate_input[:, lanes].astype(f32))
        normed.append((attended * lax.rsqrt(squares + epsilon) * gain[:, lanes] * gating).astype(bf16))
    normed = jnp.concatenate(normed, axis=1)
    peers, _, width = out.shape
    for c in range(0, peers, 2):
        product = mm(normed, weight[:, c * width:(c + 2) * width])
        out[c] = product[:, :width].astype(bf16)
        out[c + 1] = product[:, width:].astype(bf16)


def slots_of(ids, experts, capacity):
    positions = ids.shape[1]
    expert = lax.broadcasted_iota(jnp.int32, (experts, positions), 0)
    choices = [(ids[k:k + 1, :] == expert).astype(f32) for k in range(2)]
    earlier = mm((choices[0] + choices[1]).astype(bf16), lower_triangle(positions, True).astype(bf16), 1, 1)
    slot = lax.broadcasted_iota(jnp.int32, (experts * capacity, positions), 0)
    found = []
    for k, choice in enumerate(choices):
        position = jnp.sum(choice * earlier, axis=0, keepdims=True).astype(jnp.int32)
        found.append((slot == ids[k:k + 1, :] * capacity + position).astype(f32))
    return found


def prepare_kernel(place, gain, layer_input, ids, scale, layer, chosen, *, experts, capacity):
    scale[...] = gain[place[0]]
    layer[...] = layer_input[...]
    first, second = slots_of(ids[...], experts, capacity)
    chosen[...] = (first + second).astype(bf16)


def dispatch_kernel(partial, scale, layer, chosen, outgoing, hidden):
    total = layer[...].astype(f32)
    for k in range(partial.shape[0]):
        total += partial[k].astype(f32)
    hidden[...] = total
    outgoing[...] = mm(chosen[...], (total * scale[...]).astype(bf16)).astype(bf16)


def fetch(pairs, sems):
    copies = [pltpu.make_async_copy(source, target, sems.at[k]) for k, (source, target) in enumerate(pairs)]
    for copy in copies:
        copy.start()
    return copies


def load_kernel(source, target, sems):
    parts = sems.shape[0]
    rows = source.shape[0] // parts
    pairs = [(source.at[pl.ds(k * rows, rows)], target.at[pl.ds(k * rows, rows)]) for k in range(parts)]
    for copy in fetch(pairs, sems):
        copy.wait()


def row_copies(place, weights, gate_up, sems, order, peers):
    depth, share = weights[0].shape
    rows = depth // peers
    copies = []
    for c, distance in enumerate(order):
        start = pl.multiple_of(lax.rem(place[0] + distance + peers, peers) * rows, rows)
        for k, weight in enumerate(weights):
            target = gate_up.at[pl.ds(c * rows, rows), pl.ds(k * share, share)]
            copies.append(pltpu.make_async_copy(weight.at[pl.ds(start, rows)], target, sems.at[c * len(weights) + k]))
    return copies


def column_copies(place, weights, down, sems, order, peers):
    share, depth = weights[0].shape
    width = depth // peers
    copies = []
    for c, distance in enumerate(order):
        start = pl.multiple_of(lax.rem(place[0] + distance + peers, peers) * width, width)
        for k, weight in enumerate(weights):
            target = down.at[pl.ds(k * share, share), pl.ds(c * width, width)]
            copies.append(pltpu.make_async_copy(weight.at[:, pl.ds(start, width)], target, sems.at[c * len(weights) + k]))
    return copies


def gate_up_sums(place, pieces, inverse, router, gate_up, order):
    peers, _, width = inverse.shape
    experts = router.shape[0]
    squares, logits = 0.0, 0.0
    for k, piece in enumerate(pieces):
        group = lax.rem(place[0] + order[k] + peers, peers)
        wide = piece.astype(f32) * inverse[group]
        squares += jnp.sum(wide * wide, axis=1, keepdims=True)
        logits += mm(piece, router[:, pl.ds(pl.multiple_of(group * width, width), width)], 1, 1)
    total = mm(jnp.concatenate(pieces, axis=1), gate_up[...])
    beside = jnp.concatenate([logits, jnp.broadcast_to(squares, (logits.shape[0], 128 - experts))], axis=1)
    return total, beside


def pair_sums_kernel(place, inverse, router, gate_up, *refs, order, rows, columns, fresh):
    weights, downs, chunks = refs[:4], refs[4:6], refs[6:10]
    befores, outs = ((), refs[10:]) if fresh else (refs[10:14], refs[14:])
    peers = inverse.shape[0]
    totals, loaded, sems = outs[:4], outs[4:-2], outs[-2:]
    copies = row_copies(place, weights, loaded[0], sems[0], rows, peers)
    if columns:
        copies += column_copies(place, downs, loaded[1], sems[1], columns, peers)
    for copy in copies:
        copy.start()
    for h in range(2):
        found = gate_up_sums(place, [ref[...] for ref in chunks[2 * h:2 * h + 2]], inverse, router, gate_up, order)
        for k in range(2):
            totals[2 * h + k][...] = found[k] if fresh else befores[2 * h + k][...] + found[k]
    for copy in copies:
        copy.wait()


def first_load_kernel(place, gain, router, others, *refs, rows, columns):
    weights, downs, (gate_up, down, inverse, router_out, others_out, *sems) = refs[:4], refs[4:6], refs[6:]
    peers = gain.shape[0]
    copies = row_copies(place, weights, gate_up, sems[0], rows, peers)
    copies += column_copies(place, downs, down, sems[1], columns, peers)
    for copy in copies:
        copy.start()
    inverse[...] = 1.0 / gain[...]
    router_out[...] = router[...]
    others_out[...] = others[...]
    for copy in copies:
        copy.wait()


def mixing_of(place, others, logits, h, capacity):
    rows, experts = logits.shape
    blocks, lanes = others.shape
    row = lax.broadcasted_iota(jnp.int32, (rows, blocks), 0)
    block = lax.broadcasted_iota(jnp.int32, (rows, blocks), 1)
    sender = 2 * (lax.div(row, capacity) + h * (rows // capacity)) + place[1]
    from_sender = mm((sender == block).astype(bf16), others[...].astype(bf16))
    row = lax.broadcasted_iota(jnp.int32, (rows, lanes), 0)
    lane = lax.broadcasted_iota(jnp.int32, (rows, lanes), 1)
    own_lane = lax.rem(place[2], lanes // capacity) * capacity + lax.rem(row, capacity)
    other = jnp.sum(jnp.where(lane == own_lane, from_sender, 0.0), axis=1, keepdims=True).astype(jnp.int32)
    expert = lax.broadcasted_iota(jnp.int32, (rows, experts), 1)
    sign = (expert == place[2]).astype(f32) - (expert == other).astype(f32)
    return jax.nn.sigmoid(jnp.sum(sign * logits, axis=1, keepdims=True))


def products(activated, down, start, count, share):
    found = []
    for c in range(start, start + count, 2):
        both = min(2, start + count - c)
        product = mm(activated, down[:, c * share:(c + both) * share])
        found += [product[:, k * share:(k + 1) * share].astype(bf16) for k in range(both)]
    return found


def far_products_kernel(
    place, inverse, router, gate_up, down, others, total, beside, *refs, order, h, far, width, capacity
):
    count = len(order)
    outs, activated = refs[count:-1], refs[-1]
    units = activated.shape[1]
    product, sums = gate_up_sums(place, [ref[...] for ref in refs[:count]], inverse, router, gate_up, order)
    sums += beside[...]
    experts = router.shape[0]
    scale = lax.rsqrt(sums[:, experts:experts + 1] / width + epsilon)
    mixing = mixing_of(place, others, sums[:, :experts] * scale, h, capacity)
    both = (total[...] + product) * scale
    gated = both[:, :units]
    active = (gated * jax.nn.sigmoid(gated) * both[:, units:] * mixing).astype(bf16)
    activated[...] = active
    for k, piece in enumerate(products(active, down, 0, far, outs[0].shape[1])):
        outs[k][...] = piece


def near_products_kernel(active_a, active_b, down, *outs, near):
    for h, active in enumerate((active_a, active_b)):
        for k, piece in enumerate(products(active[...], down, 0, near, outs[0].shape[1])):
            outs[2 * k + h][...] = piece


def combine_kernel(returned, hidden, chosen, out):
    out[...] = (hidden[...] + mm(chosen[...], returned[...], 0, 0)).astype(out.dtype)


def call(kernel, shapes, *args, **kwargs):
    return pl.pallas_call(
        kernel,
        out_shape=shapes,
        compiler_params=pltpu.CompilerParams(vmem_limit_bytes=LIMIT),
        **kwargs,
    )(*args)


def stays(x):
    return pltpu.with_memory_space_constraint(x, pltpu.HBM)


def in_vmem(x):
    return pltpu.with_memory_space_constraint(x, pltpu.VMEM)


def whole(shape):
    return pl.BlockSpec(shape, lambda *_: (0,) * len(shape))


def shards(
    layer_input, queries, keys, values, gate_input, log_decay, prior_state, attn_gain,
    out_weight, moe_gain, router, expert_ids, w_gate, w_up, w_down,
):
    struct = jax.ShapeDtypeStruct
    positions, head_lanes = queries.shape
    heads, size, _ = prior_state.shape
    chips, cores, peers = lax.axis_size("chip"), lax.axis_size("core"), lax.axis_size("tp")
    blocks = chips * cores
    width = out_weight.shape[1]
    share = layer_input.shape[1]
    experts = router.shape[1]
    capacity = 8 * positions // blocks
    slots = experts * capacity
    core, chip, tp = lax.axis_index("core"), lax.axis_index("chip"), lax.axis_index("tp")
    cx = chip * cores + core
    place = jnp.stack([tp, core, chip])
    place, cx, tp, keys = lax.optimization_barrier((place, cx, tp, keys))

    ids = stays(expert_ids.T)
    queries, keys, values, log_decay = stays(queries), stays(keys), stays(values), stays(log_decay)
    vmem = pl.BlockSpec(memory_space=pltpu.VMEM)
    smem = pl.BlockSpec(memory_space=pltpu.SMEM)
    tied = lax.optimization_barrier

    def moved(piece, step):
        return lax.ppermute(piece, "tp", [(i, (i + step) % peers) for i in range(peers)])

    def plus(*pieces):
        return sum(piece.astype(f32) for piece in pieces).astype(bf16)
    hbm = pl.BlockSpec(memory_space=pl.ANY)

    swap = [(0, 1), (1, 0)]
    weights = []
    for weight in (w_gate[0], w_up[0], w_down[0]):
        weights += [weight, lax.ppermute(weight, "core", swap)]

    rows = heads * size // blocks
    parts = call(
        functools.partial(block_state_kernel, experts=experts, capacity=capacity),
        struct((heads, size // rows, 2 * rows, size), bf16), keys, values, log_decay, ids,
    )
    parts, out_weight, prior_state = lax.optimization_barrier((parts, out_weight, prior_state))
    prior = pl.pallas_call(
        load_part_kernel,
        out_shape=pltpu.VMEM((rows, size), f32),
        in_specs=[smem, hbm],
        out_specs=vmem,
        scratch_shapes=[pltpu.SemaphoreType.DMA],
        compiler_params=pltpu.CompilerParams(vmem_limit_bytes=4 << 20),
        cost_estimate=pl.CostEstimate(flops=0, bytes_accessed=1 << 20, transcendentals=0),
    )(cx.reshape(1), stays(prior_state.reshape(heads * size, size)))
    out_weight = pl.pallas_call(
        load_kernel,
        out_shape=pltpu.VMEM((head_lanes, width), bf16),
        in_specs=[hbm],
        out_specs=vmem,
        scratch_shapes=[pltpu.SemaphoreType.DMA((4,))],
        compiler_params=pltpu.CompilerParams(vmem_limit_bytes=4 << 20),
        cost_estimate=pl.CostEstimate(flops=0, bytes_accessed=2 * head_lanes * width, transcendentals=0),
    )(stays(out_weight))
    received = lax.all_to_all(parts.reshape(blocks, 2 * rows, size), ("chip", "core"), 0, 0, tiled=True)
    inner, growth = call(
        inner_kernel,
        (struct((positions, head_lanes), f32), struct((positions, heads), f32)),
        queries, keys, values, log_decay,
    )
    befores, others = call(
        state_scan_kernel, (struct((blocks, rows, size), bf16), pltpu.HBM((blocks, size), f32)),
        received, in_vmem(prior), in_specs=[vmem] * 2,
    )
    state = lax.all_to_all(befores, ("chip", "core"), 0, 0, tiled=True).reshape(heads * size, size)

    partial = call(
        functools.partial(project_kernel, heads=heads), struct((peers, positions, share), bf16),
        queries, stays(inner), stays(growth), state, stays(gate_input), stays(attn_gain.reshape(1, head_lanes)),
        in_vmem(out_weight), in_specs=[vmem] * 7,
    )
    gain_rows = moe_gain.reshape(peers, 1, share)
    partial, layer_input, ids, gain_rows = tied((partial, layer_input, ids, gain_rows))
    partial = lax.all_to_all(partial, "tp", 0, 0, tiled=True)
    small = pltpu.CompilerParams(vmem_limit_bytes=8 << 20)
    scale, layer, chosen = pl.pallas_call(
        functools.partial(prepare_kernel, experts=experts, capacity=capacity),
        out_shape=(pltpu.VMEM((1, share), f32), pltpu.VMEM((positions, share), bf16), pltpu.VMEM((slots, positions), bf16)),
        in_specs=[smem] + [vmem] * 3,
        out_specs=(vmem,) * 3,
        compiler_params=small,
    )(place, stays(gain_rows), stays(layer_input), stays(ids))
    chosen = in_vmem(chosen)
    outgoing, hidden = pl.pallas_call(
        dispatch_kernel,
        out_shape=(struct((slots, share), bf16), pltpu.VMEM((positions, share), f32)),
        in_specs=[vmem] * 4,
        out_specs=(vmem,) * 2,
        compiler_params=small,
    )(partial, in_vmem(scale), in_vmem(layer), chosen)

    arrived = lax.all_to_all(outgoing.reshape(chips, capacity, share), "chip", 0, 0, tiled=True)
    held = chips * capacity
    half = held // 2
    arrived = arrived.reshape(held, share)
    here = (arrived[:half], arrived[half:])
    here, weights = lax.optimization_barrier((here, weights))

    order = (0, 1, -1, 2, -2, 3, -3, 4)
    parts = order[:2], order[2:4], order[4:6], order[6:]
    far, near = (4, 3, -3), (2, -2, 1, -1, 0)
    units = cores * share
    work = held * width * units
    params = pltpu.CompilerParams(vmem_limit_bytes=LIMIT)
    gain, router = stays(moe_gain.reshape(peers, 1, share)), stays(router.T)
    others = stays(others)
    sides, downs = [stays(weight) for weight in weights[:4]], [stays(weight) for weight in weights[4:]]

    def cost(flops, size):
        return pl.CostEstimate(flops=flops, bytes_accessed=size, transcendentals=0)

    def kept(kernel, shapes, flops, specs, args, scratch=(), **options):
        return pl.pallas_call(
            functools.partial(kernel, **options),
            out_shape=shapes,
            in_specs=specs + [vmem] * (len(args) - len(specs)),
            out_specs=(vmem,) * len(shapes),
            scratch_shapes=scratch,
            compiler_params=params,
            cost_estimate=cost(flops, 4 << 20),
        )(*args)

    sums = (struct((half, 2 * units), f32), struct((half, 128), f32)) * 2
    wide = pltpu.VMEM((width // 4, 2 * units), bf16)
    semaphores = [pltpu.SemaphoreType.DMA((8,)), pltpu.SemaphoreType.DMA((2 * peers,))]
    got = ({0: here[0]}, {0: here[1]})
    for distance in (1, 2, 3):
        moving = [(moved(mine[1 - distance], 1), moved(mine[distance - 1], -1)) for mine in got]
        chunks = [mine[k] for mine in got for k in parts[distance - 2]] if distance > 1 else []
        if distance == 1:
            loaded = kept(
                first_load_kernel,
                (wide, pltpu.VMEM((units, len(far) * share), bf16), pltpu.VMEM(gain.shape, f32),
                 pltpu.VMEM(router.shape, bf16), pltpu.VMEM(others.shape, f32)),
                0, [smem] + [vmem] * 3 + [hbm] * 6, [place, gain, router, others, *sides, *downs], semaphores,
                rows=parts[0], columns=far,
            )
        elif distance == 2:
            *totals, gate_up, down_near = loaded = kept(
                pair_sums_kernel, sums + (wide, pltpu.VMEM((units, len(near) * share), bf16)), work,
                [smem] + [vmem] * 3 + [hbm] * 6, [place, inverse, router, in_vmem(gate_up), *sides, *downs, *chunks], semaphores,
                order=parts[0], rows=parts[1], columns=near, fresh=True,
            )
        else:
            *totals, gate_up = loaded = kept(
                pair_sums_kernel, sums + (wide,), work,
                [smem] + [vmem] * 3 + [hbm] * 6, [place, inverse, router, in_vmem(gate_up), *sides, *downs, *chunks, *totals],
                semaphores, order=parts[1], rows=parts[2], columns=(), fresh=False,
            )
        moving[0], loaded = tied((moving[0], loaded))
        if distance == 1:
            gate_up, down_far, *small = loaded
            inverse, router, others = [in_vmem(x) for x in small]
        elif distance == 2:
            *totals, gate_up, down_near = loaded
        else:
            *totals, gate_up = loaded
        for mine, (up, down_way) in zip(got, moving):
            mine[-distance], mine[distance] = lax.optimization_barrier((up, down_way))
    got[0][4], got[1][4] = moved(got[0][-3], 1), moved(got[1][3], -1)
    *totals, gate_up_last = kept(
        pair_sums_kernel, sums + (wide,), work, [smem] + [vmem] * 3 + [hbm] * 6,
        [place, inverse, router, in_vmem(gate_up), *sides, *downs, *[mine[k] for mine in got for k in parts[2]], *totals],
        semaphores, order=parts[2], rows=parts[3], columns=(), fresh=False,
    )
    gate_up_last, down_far, down_near = in_vmem(gate_up_last), in_vmem(down_far), in_vmem(down_near)
    piece = struct((half, share), bf16)
    ready = [
        kept(
            far_products_kernel, (piece,) * len(far) + (struct((half, units), bf16),), work, [smem],
            [place, inverse, router, gate_up_last, down_far, others, *totals[2 * h:2 * h + 2], *[got[h][k] for k in parts[3]]],
            order=parts[3], h=h, far=len(far), width=width, capacity=capacity,
        )
        for h in range(2)
    ]
    (a4, a3, a3m, active_a), (b4, b3, b3m, active_b) = ready

    a_up, a_down = tied((moved(a4, 1), moved(a3m, -1)))
    b_up, b_down = tied((moved(b3, 1), moved(b4, -1)))
    a2, b2, a2m, b2m, a1, b1, a1m, b1m, a0, b0 = kept(
        near_products_kernel, (piece,) * (2 * len(near)), work, [], [active_a, active_b, down_near], near=len(near))
    a_up, a_down = tied((moved(plus(a_up, a3), 1), moved(plus(a_down, a2m), -1)))
    b_up, b_down = tied((moved(plus(b_up, b2), 1), moved(plus(b_down, b3m), -1)))
    a_up, a_down = tied((moved(plus(a_up, a2), 1), moved(plus(a_down, a1m), -1)))
    b_up, b_down = tied((moved(plus(b_up, b1), 1), moved(plus(b_down, b2m), -1)))
    a_up, b_down = moved(plus(a_up, a1), 1), moved(plus(b_down, b1m), -1)
    summed = jnp.concatenate([plus(a0, a_up, a_down), plus(b0, b_up, b_down)])
    returned = lax.all_to_all(summed.reshape(chips, capacity, share), "chip", 0, 0, tiled=True)
    return call(
        combine_kernel, struct((positions, share), bf16),
        returned.reshape(slots, share), in_vmem(hidden), chosen, in_specs=[vmem] * 3,
    )


def solution(mesh):
    cx, tp = mesh.devices.shape
    fine = Mesh(mesh.devices.reshape(cx // 2, 2, tp), ("chip", "core", "tp"))
    both = ("chip", "core")
    placed = (
        P(both, "tp"), P(both, "tp"), P(both, "tp"), P(both, "tp"), P(both, "tp"),
        P("tp", both), P("tp", None, None), P("tp"), P("tp", None), P(), P(),
        P(both, None), P(both, None, "tp"), P(both, None, "tp"), P(both, "tp", None),
    )
    return jax.shard_map(shards, mesh=fine, in_specs=placed, out_specs=P(both, "tp"), check_vma=False)
```

profile of v0, /device:TPU:2, one launch (start us, length us, event | category | flops | bytes accessed | tf_op | source)
XLA Modules:
  0.0 172.7 jit_solution(4549319932830153908)
XLA Ops:
  2.3 7.6 %all-to-all-start = ((bf16[32,32,128]{2,1,0:T(8,128)(2,1)}), bf16[32,32,128]{2,1,0:T(8,128)(2,1)S(1)}, u32[]{:S(2)}, u32[]{:S(2)}) async-start(bf16[32,32,128]{2,1,0:T(8,128)(2,1)} %bitcast.4), calls=%async_computation | async-start | bytes 524288 | tf_op jit(solution)/shard_map/all_to_all | solution.py:355
  11.4 6.2 %all-to-all-done.received = bf16[32,32,128]{2,1,0:T(8,128)(2,1)S(1)} async-done(((bf16[32,32,128]{2,1,0:T(8,128)(2,1)}), bf16[32,32,128]{2,1,0:T(8,128)(2,1)S(1)}, u32[]{:S(2)}, u32[]{:S(2)}) %all-to-all-start) | async-done | bytes 262176 | tf_op jit(solution)/shard_map/all_to_all | solution.py:355
  18.4 5.0 %all-to-all-start.1 = ((bf16[32,16,128]{2,1,0:T(8,128)(2,1)}), bf16[32,16,128]{2,1,0:T(8,128)(2,1)S(1)}, u32[]{:S(2)}, u32[]{:S(2)}) async-start(bf16[32,16,128]{2,1,0:T(8,128)(2,1)} %get-tuple-element.124), calls=%async_computation.1 | async-start | bytes 262144 | tf_op jit(solution)/shard_map/all_to_all | solution.py:365
  33.0 8.5 %all-to-all-start.2 = ((bf16[8,128,384]{2,1,0:T(8,128)(2,1)}), bf16[8,128,384]{2,1,0:T(8,128)(2,1)S(1)}, u32[]{:S(2)}, u32[]{:S(2)}) async-start(bf16[8,128,384]{2,1,0:T(8,128)(2,1)} %copy-done), calls=%async_computation.2 | async-start | bytes 1572864 | tf_op jit(solution)/shard_map/all_to_all | solution.py:374
  42.7 22.3 %all-to-all-done.2.partial = bf16[8,128,384]{2,1,0:T(8,128)(2,1)S(1)} async-done(((bf16[8,128,384]{2,1,0:T(8,128)(2,1)}), bf16[8,128,384]{2,1,0:T(8,128)(2,1)S(1)}, u32[]{:S(2)}, u32[]{:S(2)}) %all-to-all-start.2) | async-done | bytes 786464 | tf_op jit(solution)/shard_map/all_to_all | solution.py:374
  65.2 14.5 %all_to_all.25 = bf16[16,32,384]{2,1,0:T(8,128)(2,1)S(1)} all-to-all(bf16[16,32,384]{2,1,0:T(8,128)(2,1)S(1)} %bitcast.27), channel_id=1, replica_groups=mesh['chip'=16,'core'=2,'tp'=8] {'chip'}, dimensions={0} | all-to-all | bytes 786432 | tf_op jit(solution)/shard_map/all_to_all | solution.py:392
  79.9 3.2 %collective-permute-start.8 = (bf16[256,384]{1,0:T(8,128)(2,1)S(1)}, bf16[256,384]{1,0:T(8,128)(2,1)S(1)}, u32[]{:S(2)}, u32[]{:S(2)}) collective-permute-start(bf16[256,384]{1,0:T(8,128)(2,1)S(1)} %bitcast.21), channel_id=1, source_target_pairs={{0,7},{1,0},{2,1},{3,2},{4,3},{5,4},{6,5},{7,6},{8,15},{9,8},{10,9... | collective-permute-start | bytes 589832 | tf_op jit(solution)/shard_map/ppermute | solution.py:320
  83.1 3.2 %collective-permute-start.4 = (bf16[256,384]{1,0:T(8,128)(2,1)S(1)}, bf16[256,384]{1,0:T(8,128)(2,1)S(1)}, u32[]{:S(2)}, u32[]{:S(2)}) collective-permute-start(bf16[256,384]{1,0:T(8,128)(2,1)S(1)} %bitcast.24), channel_id=1, source_target_pairs={{0,7},{1,0},{2,1},{3,2},{4,3},{5,4},{6,5},{7,6},{8,15},{9,8},{10,9... | collective-permute-start | bytes 589832 | tf_op jit(solution)/shard_map/ppermute | solution.py:320
  88.6 3.4 %collective-permute-start.12 = (bf16[256,384]{1,0:T(8,128)(2,1)S(1)}, bf16[256,384]{1,0:T(8,128)(2,1)S(1)}, u32[]{:S(2)}, u32[]{:S(2)}) collective-permute-start(bf16[256,384]{1,0:T(8,128)(2,1)S(1)} %collective-permute-done.8.refs_9_), channel_id=1, source_target_pairs={{0,7},{1,0},{2,1},{3,2},{4,3},{5,4},{6,5},{7,6},{8,15},{9,8},{10,9... | collective-permute-start | bytes 589832 | tf_op jit(solution)/shard_map/ppermute | solution.py:320
  92.0 3.3 %shard_map.153 = (bf16[768,1536]{1,0:T(8,128)(2,1)S(1)}, bf16[768,1152]{1,0:T(8,128)(2,1)S(1)}, f32[8,1,384]{2,1,0:T(1,128)S(1)}, bf16[16,3072]{1,0:T(8,128)(2,1)S(1)}, f32[32,128]{1,0:T(8,128)S(1)}) custom-call(s32[3]{0:T(128)S(1)} %pad_add_fusion.place, f32[8,1,384]{2,1,0:T(1,128)} %bitcast.47, bf16[16,3072]{1,0:T(8,128)(2,1)} %bitcast.45, ...), custom_call_target="tpu_custom_call" | custom-call | bytes 4194304 | tf_op jit(solution)/shard_map/pallas_call | solution.py:413
  95.4 3.2 %collective-permute-start.6 = (bf16[256,384]{1,0:T(8,128)(2,1)S(1)}, bf16[256,384]{1,0:T(8,128)(2,1)S(1)}, u32[]{:S(2)}, u32[]{:S(2)}) collective-permute-start(bf16[256,384]{1,0:T(8,128)(2,1)S(1)} %collective-permute-done.4.refs_7_), channel_id=1, source_target_pairs={{0,7},{1,0},{2,1},{3,2},{4,3},{5,4},{6,5},{7,6},{8,15},{9,8},{10,9... | collective-permute-start | bytes 589832 | tf_op jit(solution)/shard_map/ppermute | solution.py:320
  98.6 3.2 %collective-permute-start.14 = (bf16[256,384]{1,0:T(8,128)(2,1)S(1)}, bf16[256,384]{1,0:T(8,128)(2,1)S(1)}, u32[]{:S(2)}, u32[]{:S(2)}) collective-permute-start(bf16[256,384]{1,0:T(8,128)(2,1)S(1)} %collective-permute-done.12.refs_9_), channel_id=1, source_target_pairs={{0,7},{1,0},{2,1},{3,2},{4,3},{5,4},{6,5},{7,6},{8,15},{9,8},{10,9... | collective-permute-start | bytes 589832 | tf_op jit(solution)/shard_map/ppermute | solution.py:320
  101.9 4.5 %shard_map.154 = (f32[256,1536]{1,0:T(8,128)S(1)}, f32[256,128]{1,0:T(8,128)S(1)}, f32[256,1536]{1,0:T(8,128)S(1)}, f32[256,128]{1,0:T(8,128)S(1)}, bf16[768,153...) custom-call(s32[3]{0:T(128)S(1)} %pad_add_fusion.place, f32[8,1,384]{2,1,0:T(1,128)S(1)} %get-tuple-element.147.inverse, ...), custom_call_target="tpu_custom_call" | custom-call | flops 1207959552 | bytes 4194304 | tf_op jit(solution)/shard_map/pallas_call | solution.py:413
  106.5 3.2 %collective-permute-start.10 = (bf16[256,384]{1,0:T(8,128)(2,1)S(1)}, bf16[256,384]{1,0:T(8,128)(2,1)S(1)}, u32[]{:S(2)}, u32[]{:S(2)}) collective-permute-start(bf16[256,384]{1,0:T(8,128)(2,1)S(1)} %collective-permute-done.6.refs_7_), channel_id=1, source_target_pairs={{0,7},{1,0},{2,1},{3,2},{4,3},{5,4},{6,5},{7,6},{8,15},{9,8},{10,9... | collective-permute-start | bytes 589832 | tf_op jit(solution)/shard_map/ppermute | solution.py:320
  110.1 3.6 %shard_map.155 = (f32[256,1536]{1,0:T(8,128)S(1)}, f32[256,128]{1,0:T(8,128)S(1)}, f32[256,1536]{1,0:T(8,128)S(1)}, f32[256,128]{1,0:T(8,128)S(1)}, bf16[768,1536]{1,0:T(8,128)(2,1)S(1)}) custom-call(s32[3]{0:T(128)S(1)} %pad_add_fusion.place, f32[8,1,384]{2,1,0:T(1,128)S(1)} %get-tuple-element.147.inverse, bf16[16,3072]{1,0:T(8,128)(2,1)S(1)} %get-tuple-element.148.router, ...), custom_call_target="tpu_custom_call" | custom-call | flops 1207959552 | bytes 4194304 | tf_op jit(solution)/shard_map/pallas_call | solution.py:413
  115.4 3.6 %shard_map.156 = (f32[256,1536]{1,0:T(8,128)S(1)}, f32[256,128]{1,0:T(8,128)S(1)}, f32[256,1536]{1,0:T(8,128)S(1)}, f32[256,128]{1,0:T(8,128)S(1)}, bf16[768,1536]{1,0:T(8,128)(2,1)S(1)}) custom-call(s32[3]{0:T(128)S(1)} %pad_add_fusion.place, f32[8,1,384]{2,1,0:T(1,128)S(1)} %get-tuple-element.147.inverse, bf16[16,3072]{1,0:T(8,128)(2,1)S(1)} %get-tuple-element.148.router, ...), custom_call_target="tpu_custom_call" | custom-call | flops 1207959552 | bytes 4194304 | tf_op jit(solution)/shard_map/pallas_call | solution.py:413
  121.5 3.3 %collective-permute-start.25 = (bf16[256,384]{1,0:T(8,128)(2,1)S(1)}, bf16[256,384]{1,0:T(8,128)(2,1)S(1)}, u32[]{:S(2)}, u32[]{:S(2)}) collective-permute-start(bf16[256,384]{1,0:T(8,128)(2,1)S(1)} %get-tuple-element.216), channel_id=1, source_target_pairs={{0,7},{1,0},{2,1},{3,2},{4,3},{5,4},{6,5},{7,6},{8,15},{9,8},{10,9... | collective-permute-start | bytes 589832 | tf_op jit(solution)/shard_map/ppermute | solution.py:320
  127.2 3.2 %collective-permute-start.18 = (bf16[256,384]{1,0:T(8,128)(2,1)S(1)}, bf16[256,384]{1,0:T(8,128)(2,1)S(1)}, u32[]{:S(2)}, u32[]{:S(2)}) collective-permute-start(bf16[256,384]{1,0:T(8,128)(2,1)S(1)} %get-tuple-element.202), channel_id=1, source_target_pairs={{0,7},{1,0},{2,1},{3,2},{4,3},{5,4},{6,5},{7,6},{8,15},{9,8},{10,9... | collective-permute-start | bytes 589832 | tf_op jit(solution)/shard_map/ppermute | solution.py:320
  132.4 3.3 %collective-permute-start.27 = (bf16[256,384]{1,0:T(8,128)(2,1)S(1)}, bf16[256,384]{1,0:T(8,128)(2,1)S(1)}, u32[]{:S(2)}, u32[]{:S(2)}) collective-permute-start(bf16[256,384]{1,0:T(8,128)(2,1)S(1)} %add_convert_fusion.4), channel_id=1, source_target_pairs={{0,7},{1,0},{2,1},{3,2},{4,3},{5,4},{6,5},{7,6},{8,15},{9,8},{10,9... | collective-permute-start | bytes 589832 | tf_op jit(solution)/shard_map/ppermute | solution.py:320
  136.1 3.3 %collective-permute-start.20 = (bf16[256,384]{1,0:T(8,128)(2,1)S(1)}, bf16[256,384]{1,0:T(8,128)(2,1)S(1)}, u32[]{:S(2)}, u32[]{:S(2)}) collective-permute-start(bf16[256,384]{1,0:T(8,128)(2,1)S(1)} %add_convert_fusion.10), channel_id=1, source_target_pairs={{0,7},{1,0},{2,1},{3,2},{4,3},{5,4},{6,5},{7,6},{8,15},{9,8},{10,9... | collective-permute-start | bytes 589832 | tf_op jit(solution)/shard_map/ppermute | solution.py:320
  140.7 3.3 %collective-permute-start.29 = (bf16[256,384]{1,0:T(8,128)(2,1)S(1)}, bf16[256,384]{1,0:T(8,128)(2,1)S(1)}, u32[]{:S(2)}, u32[]{:S(2)}) collective-permute-start(bf16[256,384]{1,0:T(8,128)(2,1)S(1)} %add_convert_fusion.2), channel_id=1, source_target_pairs={{0,7},{1,0},{2,1},{3,2},{4,3},{5,4},{6,5},{7,6},{8,15},{9,8},{10,9... | collective-permute-start | bytes 589832 | tf_op jit(solution)/shard_map/ppermute | solution.py:320
  145.0 3.8 %collective-permute-start.22 = (bf16[256,384]{1,0:T(8,128)(2,1)S(1)}, bf16[256,384]{1,0:T(8,128)(2,1)S(1)}, u32[]{:S(2)}, u32[]{:S(2)}) collective-permute-start(bf16[256,384]{1,0:T(8,128)(2,1)S(1)} %add_convert_fusion.8), channel_id=1, source_target_pairs={{0,7},{1,0},{2,1},{3,2},{4,3},{5,4},{6,5},{7,6},{8,15},{9,8},{10,9... | collective-permute-start | bytes 589832 | tf_op jit(solution)/shard_map/ppermute | solution.py:320
  154.6 4.8 %collective-permute-done.23 = bf16[256,384]{1,0:T(8,128)(2,1)S(1)} collective-permute-done((bf16[256,384]{1,0:T(8,128)(2,1)S(1)}, bf16[256,384]{1,0:T(8,128)(2,1)S(1)}, u32[]{:S(2)}, u32[]{:S(2)}) %collective-permute-start.23) | collective-permute-done | bytes 196640 | tf_op jit(solution)/shard_map/ppermute | solution.py:320
  159.5 12.3 %all_to_all.26 = bf16[16,32,384]{2,1,0:T(8,128)(2,1)S(1)} all-to-all(bf16[16,32,384]{2,1,0:T(8,128)(2,1)S(1)} %bitcast.43), channel_id=1, replica_groups=mesh['chip'=16,'core'=2,'tp'=8] {'chip'}, dimensions={0} | all-to-all | bytes 786432 | tf_op jit(solution)/shard_map/all_to_all | solution.py:488
  (83 shorter events, 36.6 us)
Async XLA Ops:
  2.3 15.3 %all-to-all-start = ((bf16[32,32,128]{2,1,0:T(8,128)(2,1)}), bf16[32,32,128]{2,1,0:T(8,128)(2,1)S(1)}, u32[]{:S(2)}, u32[]{:S(2)}) async-start(bf16[32,32,128]{2,1,0:T(8,128)(2,1)} %bitcast.4), calls=%async_computation | async-start | bytes 524288 | tf_op jit(solution)/shard_map/all_to_all | solution.py:355
  10.0 69.8 %collective-permute-start = (bf16[3072,384]{1,0:T(8,128)(2,1)}, bf16[3072,384]{1,0:T(8,128)(2,1)}, u32[]{:S(2)}, u32[]{:S(2)}) collective-permute-start(bf16[3072,384]{1,0:T(8,128)(2,1)} %bitcast.28), channel_id=1, source_target_pairs={{0,8},{8,0},{1,9},{9,1},{2,10},{10,2},{3,11},{11,3},{4,12},{12,4},... | collective-permute-start | bytes 7077896 | tf_op jit(solution)/shard_map/ppermute | solution.py:329
  10.2 69.6 %collective-permute-start.1 = (bf16[3072,384]{1,0:T(8,128)(2,1)}, bf16[3072,384]{1,0:T(8,128)(2,1)}, u32[]{:S(2)}, u32[]{:S(2)}) collective-permute-start(bf16[3072,384]{1,0:T(8,128)(2,1)} %bitcast.33), channel_id=1, source_target_pairs={{0,8},{8,0},{1,9},{9,1},{2,10},{10,2},{3,11},{11,3},{4,12},{12,4},... | collective-permute-start | bytes 7077896 | tf_op jit(solution)/shard_map/ppermute | solution.py:329
  10.6 69.3 %collective-permute-start.2 = (bf16[384,3072]{1,0:T(8,128)(2,1)}, bf16[384,3072]{1,0:T(8,128)(2,1)}, u32[]{:S(2)}, u32[]{:S(2)}) collective-permute-start(bf16[384,3072]{1,0:T(8,128)(2,1)} %bitcast.38), channel_id=1, source_target_pairs={{0,8},{8,0},{1,9},{9,1},{2,10},{10,2},{3,11},{11,3},{4,12},{12,4},... | collective-permute-start | bytes 7077896 | tf_op jit(solution)/shard_map/ppermute | solution.py:329
  18.4 11.7 %all-to-all-start.1 = ((bf16[32,16,128]{2,1,0:T(8,128)(2,1)}), bf16[32,16,128]{2,1,0:T(8,128)(2,1)S(1)}, u32[]{:S(2)}, u32[]{:S(2)}) async-start(bf16[32,16,128]{2,1,0:T(8,128)(2,1)} %get-tuple-element.124), calls=%async_computation.1 | async-start | bytes 262144 | tf_op jit(solution)/shard_map/all_to_all | solution.py:365
  33.0 31.9 %all-to-all-start.2 = ((bf16[8,128,384]{2,1,0:T(8,128)(2,1)}), bf16[8,128,384]{2,1,0:T(8,128)(2,1)S(1)}, u32[]{:S(2)}, u32[]{:S(2)}) async-start(bf16[8,128,384]{2,1,0:T(8,128)(2,1)} %copy-done), calls=%async_computation.2 | async-start | bytes 1572864 | tf_op jit(solution)/shard_map/all_to_all | solution.py:374
  79.8 8.8 %collective-permute-start.7 = (bf16[256,384]{1,0:T(8,128)(2,1)S(1)}, bf16[256,384]{1,0:T(8,128)(2,1)S(1)}, u32[]{:S(2)}, u32[]{:S(2)}) collective-permute-start(bf16[256,384]{1,0:T(8,128)(2,1)S(1)} %bitcast.20), channel_id=1, source_target_pairs={{0,1},{1,2},{2,3},{3,4},{4,5},{5,6},{6,7},{7,0},{8,9},{9,10},{10,1... | collective-permute-start | bytes 589832 | tf_op jit(solution)/shard_map/ppermute | solution.py:320
  79.9 8.7 %collective-permute-start.8 = (bf16[256,384]{1,0:T(8,128)(2,1)S(1)}, bf16[256,384]{1,0:T(8,128)(2,1)S(1)}, u32[]{:S(2)}, u32[]{:S(2)}) collective-permute-start(bf16[256,384]{1,0:T(8,128)(2,1)S(1)} %bitcast.21), channel_id=1, source_target_pairs={{0,7},{1,0},{2,1},{3,2},{4,3},{5,4},{6,5},{7,6},{8,15},{9,8},{10,9... | collective-permute-start | bytes 589832 | tf_op jit(solution)/shard_map/ppermute | solution.py:320
  83.1 12.1 %collective-permute-start.3 = (bf16[256,384]{1,0:T(8,128)(2,1)S(1)}, bf16[256,384]{1,0:T(8,128)(2,1)S(1)}, u32[]{:S(2)}, u32[]{:S(2)}) collective-permute-start(bf16[256,384]{1,0:T(8,128)(2,1)S(1)} %bitcast.23), channel_id=1, source_target_pairs={{0,1},{1,2},{2,3},{3,4},{4,5},{5,6},{6,7},{7,0},{8,9},{9,10},{10,1... | collective-permute-start | bytes 589832 | tf_op jit(solution)/shard_map/ppermute | solution.py:320
  83.1 12.1 %collective-permute-start.4 = (bf16[256,384]{1,0:T(8,128)(2,1)S(1)}, bf16[256,384]{1,0:T(8,128)(2,1)S(1)}, u32[]{:S(2)}, u32[]{:S(2)}) collective-permute-start(bf16[256,384]{1,0:T(8,128)(2,1)S(1)} %bitcast.24), channel_id=1, source_target_pairs={{0,7},{1,0},{2,1},{3,2},{4,3},{5,4},{6,5},{7,6},{8,15},{9,8},{10,9... | collective-permute-start | bytes 589832 | tf_op jit(solution)/shard_map/ppermute | solution.py:320
  88.6 10.0 %collective-permute-start.11 = (bf16[256,384]{1,0:T(8,128)(2,1)S(1)}, bf16[256,384]{1,0:T(8,128)(2,1)S(1)}, u32[]{:S(2)}, u32[]{:S(2)}) collective-permute-start(bf16[256,384]{1,0:T(8,128)(2,1)S(1)} %collective-permute-done.7.refs_8_), channel_id=1, source_target_pairs={{0,1},{1,2},{2,3},{3,4},{4,5},{5,6},{6,7},{7,0},{8,9},{9,10},{10,1... | collective-permute-start | bytes 589832 | tf_op jit(solution)/shard_map/ppermute | solution.py:320
  88.6 10.0 %collective-permute-start.12 = (bf16[256,384]{1,0:T(8,128)(2,1)S(1)}, bf16[256,384]{1,0:T(8,128)(2,1)S(1)}, u32[]{:S(2)}, u32[]{:S(2)}) collective-permute-start(bf16[256,384]{1,0:T(8,128)(2,1)S(1)} %collective-permute-done.8.refs_9_), channel_id=1, source_target_pairs={{0,7},{1,0},{2,1},{3,2},{4,3},{5,4},{6,5},{7,6},{8,15},{9,8},{10,9... | collective-permute-start | bytes 589832 | tf_op jit(solution)/shard_map/ppermute | solution.py:320
  95.3 11.0 %collective-permute-start.5 = (bf16[256,384]{1,0:T(8,128)(2,1)S(1)}, bf16[256,384]{1,0:T(8,128)(2,1)S(1)}, u32[]{:S(2)}, u32[]{:S(2)}) collective-permute-start(bf16[256,384]{1,0:T(8,128)(2,1)S(1)} %collective-permute-done.3.refs_6_), channel_id=1, source_target_pairs={{0,1},{1,2},{2,3},{3,4},{4,5},{5,6},{6,7},{7,0},{8,9},{9,10},{10,1... | collective-permute-start | bytes 589832 | tf_op jit(solution)/shard_map/ppermute | solution.py:320
  95.4 11.0 %collective-permute-start.6 = (bf16[256,384]{1,0:T(8,128)(2,1)S(1)}, bf16[256,384]{1,0:T(8,128)(2,1)S(1)}, u32[]{:S(2)}, u32[]{:S(2)}) collective-permute-start(bf16[256,384]{1,0:T(8,128)(2,1)S(1)} %collective-permute-done.4.refs_7_), channel_id=1, source_target_pairs={{0,7},{1,0},{2,1},{3,2},{4,3},{5,4},{6,5},{7,6},{8,15},{9,8},{10,9... | collective-permute-start | bytes 589832 | tf_op jit(solution)/shard_map/ppermute | solution.py:320
  98.6 11.1 %collective-permute-start.13 = (bf16[256,384]{1,0:T(8,128)(2,1)S(1)}, bf16[256,384]{1,0:T(8,128)(2,1)S(1)}, u32[]{:S(2)}, u32[]{:S(2)}) collective-permute-start(bf16[256,384]{1,0:T(8,128)(2,1)S(1)} %collective-permute-done.11.refs_8_), channel_id=1, source_target_pairs={{0,1},{1,2},{2,3},{3,4},{4,5},{5,6},{6,7},{7,0},{8,9},{9,10},{10,1... | collective-permute-start | bytes 589832 | tf_op jit(solution)/shard_map/ppermute | solution.py:320
  98.6 11.1 %collective-permute-start.14 = (bf16[256,384]{1,0:T(8,128)(2,1)S(1)}, bf16[256,384]{1,0:T(8,128)(2,1)S(1)}, u32[]{:S(2)}, u32[]{:S(2)}) collective-permute-start(bf16[256,384]{1,0:T(8,128)(2,1)S(1)} %collective-permute-done.12.refs_9_), channel_id=1, source_target_pairs={{0,7},{1,0},{2,1},{3,2},{4,3},{5,4},{6,5},{7,6},{8,15},{9,8},{10,9... | collective-permute-start | bytes 589832 | tf_op jit(solution)/shard_map/ppermute | solution.py:320
  106.4 8.8 %collective-permute-start.9 = (bf16[256,384]{1,0:T(8,128)(2,1)S(1)}, bf16[256,384]{1,0:T(8,128)(2,1)S(1)}, u32[]{:S(2)}, u32[]{:S(2)}) collective-permute-start(bf16[256,384]{1,0:T(8,128)(2,1)S(1)} %collective-permute-done.5.refs_6_), channel_id=1, source_target_pairs={{0,1},{1,2},{2,3},{3,4},{4,5},{5,6},{6,7},{7,0},{8,9},{9,10},{10,1... | collective-permute-start | bytes 589832 | tf_op jit(solution)/shard_map/ppermute | solution.py:320
  106.5 8.7 %collective-permute-start.10 = (bf16[256,384]{1,0:T(8,128)(2,1)S(1)}, bf16[256,384]{1,0:T(8,128)(2,1)S(1)}, u32[]{:S(2)}, u32[]{:S(2)}) collective-permute-start(bf16[256,384]{1,0:T(8,128)(2,1)S(1)} %collective-permute-done.6.refs_7_), channel_id=1, source_target_pairs={{0,7},{1,0},{2,1},{3,2},{4,3},{5,4},{6,5},{7,6},{8,15},{9,8},{10,9... | collective-permute-start | bytes 589832 | tf_op jit(solution)/shard_map/ppermute | solution.py:320
  109.7 9.3 %collective-permute-start.16 = (bf16[256,384]{1,0:T(8,128)(2,1)S(1)}, bf16[256,384]{1,0:T(8,128)(2,1)S(1)}, u32[]{:S(2)}, u32[]{:S(2)}) collective-permute-start(bf16[256,384]{1,0:T(8,128)(2,1)S(1)} %collective-permute-done.14.refs_9_), channel_id=1, source_target_pairs={{0,7},{1,0},{2,1},{3,2},{4,3},{5,4},{6,5},{7,6},{8,15},{9,8},{10,9... | collective-permute-start | bytes 589832 | tf_op jit(solution)/shard_map/ppermute | solution.py:320
  115.1 9.6 %collective-permute-start.15 = (bf16[256,384]{1,0:T(8,128)(2,1)S(1)}, bf16[256,384]{1,0:T(8,128)(2,1)S(1)}, u32[]{:S(2)}, u32[]{:S(2)}) collective-permute-start(bf16[256,384]{1,0:T(8,128)(2,1)S(1)} %collective-permute-done.9.refs_0_), channel_id=1, source_target_pairs={{0,1},{1,2},{2,3},{3,4},{4,5},{5,6},{6,7},{7,0},{8,9},{9,10},{10,1... | collective-permute-start | bytes 589832 | tf_op jit(solution)/shard_map/ppermute | solution.py:320
  121.4 10.8 %collective-permute-start.24 = (bf16[256,384]{1,0:T(8,128)(2,1)S(1)}, bf16[256,384]{1,0:T(8,128)(2,1)S(1)}, u32[]{:S(2)}, u32[]{:S(2)}) collective-permute-start(bf16[256,384]{1,0:T(8,128)(2,1)S(1)} %get-tuple-element.215), channel_id=1, source_target_pairs={{0,1},{1,2},{2,3},{3,4},{4,5},{5,6},{6,7},{7,0},{8,9},{9,10},{10,1... | collective-permute-start | bytes 589832 | tf_op jit(solution)/shard_map/ppermute | solution.py:320
  121.5 10.7 %collective-permute-start.25 = (bf16[256,384]{1,0:T(8,128)(2,1)S(1)}, bf16[256,384]{1,0:T(8,128)(2,1)S(1)}, u32[]{:S(2)}, u32[]{:S(2)}) collective-permute-start(bf16[256,384]{1,0:T(8,128)(2,1)S(1)} %get-tuple-element.216), channel_id=1, source_target_pairs={{0,7},{1,0},{2,1},{3,2},{4,3},{5,4},{6,5},{7,6},{8,15},{9,8},{10,9... | collective-permute-start | bytes 589832 | tf_op jit(solution)/shard_map/ppermute | solution.py:320
  127.1 8.8 %collective-permute-start.17 = (bf16[256,384]{1,0:T(8,128)(2,1)S(1)}, bf16[256,384]{1,0:T(8,128)(2,1)S(1)}, u32[]{:S(2)}, u32[]{:S(2)}) collective-permute-start(bf16[256,384]{1,0:T(8,128)(2,1)S(1)} %get-tuple-element.201), channel_id=1, source_target_pairs={{0,1},{1,2},{2,3},{3,4},{4,5},{5,6},{6,7},{7,0},{8,9},{9,10},{10,1... | collective-permute-start | bytes 589832 | tf_op jit(solution)/shard_map/ppermute | solution.py:320
  127.2 8.7 %collective-permute-start.18 = (bf16[256,384]{1,0:T(8,128)(2,1)S(1)}, bf16[256,384]{1,0:T(8,128)(2,1)S(1)}, u32[]{:S(2)}, u32[]{:S(2)}) collective-permute-start(bf16[256,384]{1,0:T(8,128)(2,1)S(1)} %get-tuple-element.202), channel_id=1, source_target_pairs={{0,7},{1,0},{2,1},{3,2},{4,3},{5,4},{6,5},{7,6},{8,15},{9,8},{10,9... | collective-permute-start | bytes 589832 | tf_op jit(solution)/shard_map/ppermute | solution.py:320
  (13 other events, 79.0 us)
where the time goes:
time: 173 us
  starting transfers between devices  65.4 us (38%)
  waiting for transfers between devices  43.7 us (25%)
  Pallas kernels  33.3 us (19%)
  blocking collectives  26.8 us (15%)
  local copies, waits for them, and re-layouts  2.32 us (1%)
    ppermute x28, starting transfers between devices, moved(): lax.ppermute(piece, 'tp', [(i, (i + step) % peers) for i in range(peers)])  43.6 us
    all_to_all x1, waiting for transfers between devices, shards(): partial = lax.all_to_all(partial, 'tp', 0, 0, tiled=True)  22.3 us
    pallas_call x7, Pallas kernels, kept(): pl.pallas_call(functools.partial(kernel, **options), out_shape=shapes, in...  21.4 us
    all_to_all x1, blocking collectives, shards(): lax.all_to_all(outgoing.reshape(chips, capacity, share), 'chip', 0, 0, ti...  14.5 us
    ppermute x28, waiting for transfers between devices, moved(): lax.ppermute(piece, 'tp', [(i, (i + step) % peers) for i in range(peers)])  13.7 us
    all_to_all x1, blocking collectives, shards(): lax.all_to_all(summed.reshape(chips, capacity, share), 'chip', 0, 0, tile...  12.3 us
    all_to_all x1, starting transfers between devices, shards(): partial = lax.all_to_all(partial, 'tp', 0, 0, tiled=True)  8.48 us
    pallas_call x5, Pallas kernels, call(): pl.pallas_call(kernel, out_shape=shapes, compiler_params=pltpu.CompilerPa...  7.8 us
  transfers between devices with their start and end apart: 34, of which 11 were waited for; matrix products, arithmetic and copies ran while one was open for 0% of the time, Pallas kernels for 17%

commit v1 on v0

--- a/solution.py
+++ b/solution.py
@@ -358,20 +358,7 @@
         (struct((positions, head_lanes), f32), struct((positions, heads), f32)),
         queries, keys, values, log_decay,
     )
-    befores, others = call(
-        state_scan_kernel, (struct((blocks, rows, size), bf16), pltpu.HBM((blocks, size), f32)),
-        received, in_vmem(prior), in_specs=[vmem] * 2,
-    )
-    state = lax.all_to_all(befores, ("chip", "core"), 0, 0, tiled=True).reshape(heads * size, size)
-
-    partial = call(
-        functools.partial(project_kernel, heads=heads), struct((peers, positions, share), bf16),
-        queries, stays(inner), stays(growth), state, stays(gate_input), stays(attn_gain.reshape(1, head_lanes)),
-        in_vmem(out_weight), in_specs=[vmem] * 7,
-    )
     gain_rows = moe_gain.reshape(peers, 1, share)
-    partial, layer_input, ids, gain_rows = tied((partial, layer_input, ids, gain_rows))
-    partial = lax.all_to_all(partial, "tp", 0, 0, tiled=True)
     small = pltpu.CompilerParams(vmem_limit_bytes=8 << 20)
     scale, layer, chosen = pl.pallas_call(
         functools.partial(prepare_kernel, experts=experts, capacity=capacity),
@@ -380,6 +367,19 @@
         out_specs=(vmem,) * 3,
         compiler_params=small,
     )(place, stays(gain_rows), stays(layer_input), stays(ids))
+    befores, others = call(
+        state_scan_kernel, (struct((blocks, rows, size), bf16), pltpu.HBM((blocks, size), f32)),
+        received, in_vmem(prior), in_specs=[vmem] * 2,
+    )
+    state = lax.all_to_all(befores, ("chip", "core"), 0, 0, tiled=True).reshape(heads * size, size)
+
+    partial = call(
+        functools.partial(project_kernel, heads=heads), struct((peers, positions, share), bf16),
+        queries, stays(inner), stays(growth), state, stays(gate_input), stays(attn_gain.reshape(1, head_lanes)),
+        in_vmem(out_weight), in_specs=[vmem] * 7,
+    )
+    partial, chosen = tied((partial, chosen))
+    partial = lax.all_to_all(partial, "tp", 0, 0, tiled=True)
     chosen = in_vmem(chosen)
     outgoing, hidden = pl.pallas_call(
         dispatch_kernel,

time: 173 us -> 172 us (level)
  blocking collectives: 26.8 us -> 57.6 us
  waiting for transfers between devices: 43.7 us -> 21.7 us
  starting transfers between devices: 65.4 us -> 57.2 us
  local copies, waits for them, and re-layouts: 2.32 us -> 0.05 us
    all_to_all x0 -> x1, blocking collectives: none -> 31.7 us  [shards(): partial = lax.all_to_all(partial, 'tp', 0, 0, tiled=True)]
    all_to_all x1 -> x0, waiting for transfers between devices: 22.3 us -> none  [shards(): partial = lax.all_to_all(partial, 'tp', 0, 0, tiled=True)]
    all_to_all x1 -> x0, starting transfers between devices: 8.48 us -> none  [shards(): partial = lax.all_to_all(partial, 'tp', 0, 0, tiled=True)]
    unnamed x6 -> x4, local copies, waits for them, and re-layouts: 2.28 us -> 0.01 us
  transfers between devices with their start and end apart: 34 -> 33, of which waited for: 11 -> 10; matrix products, arithmetic and copies ran while one was open for 0% -> 0% of each run, Pallas kernels for 17% -> 18%
where the time goes in v1:
time: 172 us; the launch traced here: 171 us
  blocking collectives  57.6 us (33%)
  starting transfers between devices  57.2 us (33%)
  Pallas kernels  33.5 us (19%)
  waiting for transfers between devices  21.7 us (13%)
    ppermute x28, starting transfers between devices, moved(): lax.ppermute(piece, 'tp', [(i, (i + step) % peers) for i in range(peers)])  43.9 us
    all_to_all x1, blocking collectives, shards(): partial = lax.all_to_all(partial, 'tp', 0, 0, tiled=True)  31.7 us
    pallas_call x7, Pallas kernels, kept(): pl.pallas_call(functools.partial(kernel, **options), out_shape=shapes, in...  21.5 us
    ppermute x28, waiting for transfers between devices, moved(): lax.ppermute(piece, 'tp', [(i, (i + step) % peers) for i in range(peers)])  13.9 us
    all_to_all x1, blocking collectives, shards(): lax.all_to_all(outgoing.reshape(chips, capacity, share), 'chip', 0, 0, ti...  13.6 us
    all_to_all x1, blocking collectives, shards(): lax.all_to_all(summed.reshape(chips, capacity, share), 'chip', 0, 0, tile...  12.3 us
    pallas_call x5, Pallas kernels, call(): pl.pallas_call(kernel, out_shape=shapes, compiler_params=pltpu.CompilerPa...  7.8 us
    all_to_all x1, starting transfers between devices, shards(): lax.all_to_all(parts.reshape(blocks, 2 * rows, size), ('chip', 'core'), 0...  7.62 us
  transfers between devices with their start and end apart: 33, of which 10 were waited for; matrix products, arithmetic and copies ran while one was open for 0% of the time, Pallas kernels for 18%

profile of v1, /device:TPU:2, one launch (start us, length us, event | category | flops | bytes accessed | tf_op | source)
XLA Modules:
  0.0 171.2 jit_solution(3231832157602294467)
XLA Ops:
  2.3 7.6 %all-to-all-start = ((bf16[32,32,128]{2,1,0:T(8,128)(2,1)}), bf16[32,32,128]{2,1,0:T(8,128)(2,1)S(1)}, u32[]{:S(2)}, u32[]{:S(2)}) async-start(bf16[32,32,128]{2,1,0:T(8,128)(2,1)} %bitcast.4), calls=%async_computation | async-start | bytes 524288 | tf_op jit(solution)/shard_map/all_to_all | solution.py:355
  11.4 6.2 %all-to-all-done.received = bf16[32,32,128]{2,1,0:T(8,128)(2,1)S(1)} async-done(((bf16[32,32,128]{2,1,0:T(8,128)(2,1)}), bf16[32,32,128]{2,1,0:T(8,128)(2,1)S(1)}, u32[]{:S(2)}, u32[]{:S(2)}) %all-to-all-start) | async-done | bytes 262176 | tf_op jit(solution)/shard_map/all_to_all | solution.py:355
  18.4 5.0 %all-to-all-start.1 = ((bf16[32,16,128]{2,1,0:T(8,128)(2,1)}), bf16[32,16,128]{2,1,0:T(8,128)(2,1)S(1)}, u32[]{:S(2)}, u32[]{:S(2)}) async-start(bf16[32,16,128]{2,1,0:T(8,128)(2,1)} %get-tuple-element.122), calls=%async_computation.1 | async-start | bytes 262144 | tf_op jit(solution)/shard_map/all_to_all | solution.py:374
  32.0 31.7 %all_to_all.25.partial = bf16[8,128,384]{2,1,0:T(8,128)(2,1)S(1)} all-to-all(bf16[8,128,384]{2,1,0:T(8,128)(2,1)S(1)} %shard_map.150), channel_id=1, replica_groups=mesh['chip'=16,'core'=2,'tp'=8] {'tp'}, dimensions={0} | all-to-all | bytes 1572864 | tf_op jit(solution)/shard_map/all_to_all | solution.py:382
  64.1 13.6 %all_to_all.26 = bf16[16,32,384]{2,1,0:T(8,128)(2,1)S(1)} all-to-all(bf16[16,32,384]{2,1,0:T(8,128)(2,1)S(1)} %bitcast.27), channel_id=1, replica_groups=mesh['chip'=16,'core'=2,'tp'=8] {'chip'}, dimensions={0} | all-to-all | bytes 786432 | tf_op jit(solution)/shard_map/all_to_all | solution.py:392
  78.4 2.7 %collective-permute-start.8 = (bf16[256,384]{1,0:T(8,128)(2,1)S(1)}, bf16[256,384]{1,0:T(8,128)(2,1)S(1)}, u32[]{:S(2)}, u32[]{:S(2)}) collective-permute-start(bf16[256,384]{1,0:T(8,128)(2,1)S(1)} %bitcast.21), channel_id=1, source_target_pairs={{0,7},{1,0},{2,1},{3,2},{4,3},{5,4},{6,5},{7,6},{8,15},{9,8},{10,9... | collective-permute-start | bytes 589832 | tf_op jit(solution)/shard_map/ppermute | solution.py:320
  81.1 3.2 %collective-permute-start.4 = (bf16[256,384]{1,0:T(8,128)(2,1)S(1)}, bf16[256,384]{1,0:T(8,128)(2,1)S(1)}, u32[]{:S(2)}, u32[]{:S(2)}) collective-permute-start(bf16[256,384]{1,0:T(8,128)(2,1)S(1)} %bitcast.24), channel_id=1, source_target_pairs={{0,7},{1,0},{2,1},{3,2},{4,3},{5,4},{6,5},{7,6},{8,15},{9,8},{10,9... | collective-permute-start | bytes 589832 | tf_op jit(solution)/shard_map/ppermute | solution.py:320
  86.8 3.3 %collective-permute-start.12 = (bf16[256,384]{1,0:T(8,128)(2,1)S(1)}, bf16[256,384]{1,0:T(8,128)(2,1)S(1)}, u32[]{:S(2)}, u32[]{:S(2)}) collective-permute-start(bf16[256,384]{1,0:T(8,128)(2,1)S(1)} %collective-permute-done.8.refs_9_), channel_id=1, source_target_pairs={{0,7},{1,0},{2,1},{3,2},{4,3},{5,4},{6,5},{7,6},{8,15},{9,8},{10,9... | collective-permute-start | bytes 589832 | tf_op jit(solution)/shard_map/ppermute | solution.py:320
  90.1 3.3 %shard_map.153 = (bf16[768,1536]{1,0:T(8,128)(2,1)S(1)}, bf16[768,1152]{1,0:T(8,128)(2,1)S(1)}, f32[8,1,384]{2,1,0:T(1,128)S(1)}, bf16[16,3072]{1,0:T(8,128)(2,1)S(1)}, f32[32,128]{1,0:T(8,128)S(1)}) custom-call(s32[3]{0:T(128)S(1)} %pad_add_fusion.place, f32[8,1,384]{2,1,0:T(1,128)} %bitcast.47, bf16[16,3072]{1,0:T(8,128)(2,1)} %bitcast.45, ...), custom_call_target="tpu_custom_call" | custom-call | bytes 4194304 | tf_op jit(solution)/shard_map/pallas_call | solution.py:413
  93.5 3.2 %collective-permute-start.6 = (bf16[256,384]{1,0:T(8,128)(2,1)S(1)}, bf16[256,384]{1,0:T(8,128)(2,1)S(1)}, u32[]{:S(2)}, u32[]{:S(2)}) collective-permute-start(bf16[256,384]{1,0:T(8,128)(2,1)S(1)} %collective-permute-done.4.refs_7_), channel_id=1, source_target_pairs={{0,7},{1,0},{2,1},{3,2},{4,3},{5,4},{6,5},{7,6},{8,15},{9,8},{10,9... | collective-permute-start | bytes 589832 | tf_op jit(solution)/shard_map/ppermute | solution.py:320
  96.7 3.2 %collective-permute-start.14 = (bf16[256,384]{1,0:T(8,128)(2,1)S(1)}, bf16[256,384]{1,0:T(8,128)(2,1)S(1)}, u32[]{:S(2)}, u32[]{:S(2)}) collective-permute-start(bf16[256,384]{1,0:T(8,128)(2,1)S(1)} %collective-permute-done.12.refs_9_), channel_id=1, source_target_pairs={{0,7},{1,0},{2,1},{3,2},{4,3},{5,4},{6,5},{7,6},{8,15},{9,8},{10,9... | collective-permute-start | bytes 589832 | tf_op jit(solution)/shard_map/ppermute | solution.py:320
  99.9 4.5 %shard_map.154 = (f32[256,1536]{1,0:T(8,128)S(1)}, f32[256,128]{1,0:T(8,128)S(1)}, f32[256,1536]{1,0:T(8,128)S(1)}, f32[256,128]{1,0:T(8,128)S(1)}, bf16[768,153...) custom-call(s32[3]{0:T(128)S(1)} %pad_add_fusion.place, f32[8,1,384]{2,1,0:T(1,128)S(1)} %get-tuple-element.143.inverse, ...), custom_call_target="tpu_custom_call" | custom-call | flops 1207959552 | bytes 4194304 | tf_op jit(solution)/shard_map/pallas_call | solution.py:413
  104.6 3.2 %collective-permute-start.10 = (bf16[256,384]{1,0:T(8,128)(2,1)S(1)}, bf16[256,384]{1,0:T(8,128)(2,1)S(1)}, u32[]{:S(2)}, u32[]{:S(2)}) collective-permute-start(bf16[256,384]{1,0:T(8,128)(2,1)S(1)} %collective-permute-done.6.refs_7_), channel_id=1, source_target_pairs={{0,7},{1,0},{2,1},{3,2},{4,3},{5,4},{6,5},{7,6},{8,15},{9,8},{10,9... | collective-permute-start | bytes 589832 | tf_op jit(solution)/shard_map/ppermute | solution.py:320
  108.9 3.6 %shard_map.155 = (f32[256,1536]{1,0:T(8,128)S(1)}, f32[256,128]{1,0:T(8,128)S(1)}, f32[256,1536]{1,0:T(8,128)S(1)}, f32[256,128]{1,0:T(8,128)S(1)}, bf16[768,1536]{1,0:T(8,128)(2,1)S(1)}) custom-call(s32[3]{0:T(128)S(1)} %pad_add_fusion.place, f32[8,1,384]{2,1,0:T(1,128)S(1)} %get-tuple-element.143.inverse, bf16[16,3072]{1,0:T(8,128)(2,1)S(1)} %get-tuple-element.144.router, ...), custom_call_target="tpu_custom_call" | custom-call | flops 1207959552 | bytes 4194304 | tf_op jit(solution)/shard_map/pallas_call | solution.py:413
  113.5 3.6 %shard_map.156 = (f32[256,1536]{1,0:T(8,128)S(1)}, f32[256,128]{1,0:T(8,128)S(1)}, f32[256,1536]{1,0:T(8,128)S(1)}, f32[256,128]{1,0:T(8,128)S(1)}, bf16[768,1536]{1,0:T(8,128)(2,1)S(1)}) custom-call(s32[3]{0:T(128)S(1)} %pad_add_fusion.place, f32[8,1,384]{2,1,0:T(1,128)S(1)} %get-tuple-element.143.inverse, bf16[16,3072]{1,0:T(8,128)(2,1)S(1)} %get-tuple-element.144.router, ...), custom_call_target="tpu_custom_call" | custom-call | flops 1207959552 | bytes 4194304 | tf_op jit(solution)/shard_map/pallas_call | solution.py:413
  119.6 3.2 %collective-permute-start.25 = (bf16[256,384]{1,0:T(8,128)(2,1)S(1)}, bf16[256,384]{1,0:T(8,128)(2,1)S(1)}, u32[]{:S(2)}, u32[]{:S(2)}) collective-permute-start(bf16[256,384]{1,0:T(8,128)(2,1)S(1)} %get-tuple-element.212), channel_id=1, source_target_pairs={{0,7},{1,0},{2,1},{3,2},{4,3},{5,4},{6,5},{7,6},{8,15},{9,8},{10,9... | collective-permute-start | bytes 589832 | tf_op jit(solution)/shard_map/ppermute | solution.py:320
  125.3 3.2 %collective-permute-start.18 = (bf16[256,384]{1,0:T(8,128)(2,1)S(1)}, bf16[256,384]{1,0:T(8,128)(2,1)S(1)}, u32[]{:S(2)}, u32[]{:S(2)}) collective-permute-start(bf16[256,384]{1,0:T(8,128)(2,1)S(1)} %get-tuple-element.198), channel_id=1, source_target_pairs={{0,7},{1,0},{2,1},{3,2},{4,3},{5,4},{6,5},{7,6},{8,15},{9,8},{10,9... | collective-permute-start | bytes 589832 | tf_op jit(solution)/shard_map/ppermute | solution.py:320
  130.5 3.3 %collective-permute-start.27 = (bf16[256,384]{1,0:T(8,128)(2,1)S(1)}, bf16[256,384]{1,0:T(8,128)(2,1)S(1)}, u32[]{:S(2)}, u32[]{:S(2)}) collective-permute-start(bf16[256,384]{1,0:T(8,128)(2,1)S(1)} %add_convert_fusion.4), channel_id=1, source_target_pairs={{0,7},{1,0},{2,1},{3,2},{4,3},{5,4},{6,5},{7,6},{8,15},{9,8},{10,9... | collective-permute-start | bytes 589832 | tf_op jit(solution)/shard_map/ppermute | solution.py:320
  134.0 3.3 %collective-permute-start.20 = (bf16[256,384]{1,0:T(8,128)(2,1)S(1)}, bf16[256,384]{1,0:T(8,128)(2,1)S(1)}, u32[]{:S(2)}, u32[]{:S(2)}) collective-permute-start(bf16[256,384]{1,0:T(8,128)(2,1)S(1)} %add_convert_fusion.10), channel_id=1, source_target_pairs={{0,7},{1,0},{2,1},{3,2},{4,3},{5,4},{6,5},{7,6},{8,15},{9,8},{10,9... | collective-permute-start | bytes 589832 | tf_op jit(solution)/shard_map/ppermute | solution.py:320
  139.4 3.6 %collective-permute-start.29 = (bf16[256,384]{1,0:T(8,128)(2,1)S(1)}, bf16[256,384]{1,0:T(8,128)(2,1)S(1)}, u32[]{:S(2)}, u32[]{:S(2)}) collective-permute-start(bf16[256,384]{1,0:T(8,128)(2,1)S(1)} %add_convert_fusion.2), channel_id=1, source_target_pairs={{0,7},{1,0},{2,1},{3,2},{4,3},{5,4},{6,5},{7,6},{8,15},{9,8},{10,9... | collective-permute-start | bytes 589832 | tf_op jit(solution)/shard_map/ppermute | solution.py:320
  143.4 3.8 %collective-permute-start.22 = (bf16[256,384]{1,0:T(8,128)(2,1)S(1)}, bf16[256,384]{1,0:T(8,128)(2,1)S(1)}, u32[]{:S(2)}, u32[]{:S(2)}) collective-permute-start(bf16[256,384]{1,0:T(8,128)(2,1)S(1)} %add_convert_fusion.8), channel_id=1, source_target_pairs={{0,7},{1,0},{2,1},{3,2},{4,3},{5,4},{6,5},{7,6},{8,15},{9,8},{10,9... | collective-permute-start | bytes 589832 | tf_op jit(solution)/shard_map/ppermute | solution.py:320
  150.9 3.1 %collective-permute-done.30 = bf16[256,384]{1,0:T(8,128)(2,1)S(1)} collective-permute-done((bf16[256,384]{1,0:T(8,128)(2,1)S(1)}, bf16[256,384]{1,0:T(8,128)(2,1)S(1)}, u32[]{:S(2)}, u32[]{:S(2)}) %collective-permute-start.30) | collective-permute-done | bytes 196640 | tf_op jit(solution)/shard_map/ppermute | solution.py:320
  154.1 3.8 %collective-permute-done.23 = bf16[256,384]{1,0:T(8,128)(2,1)S(1)} collective-permute-done((bf16[256,384]{1,0:T(8,128)(2,1)S(1)}, bf16[256,384]{1,0:T(8,128)(2,1)S(1)}, u32[]{:S(2)}, u32[]{:S(2)}) %collective-permute-start.23) | collective-permute-done | bytes 196640 | tf_op jit(solution)/shard_map/ppermute | solution.py:320
  158.0 12.3 %all_to_all.27 = bf16[16,32,384]{2,1,0:T(8,128)(2,1)S(1)} all-to-all(bf16[16,32,384]{2,1,0:T(8,128)(2,1)S(1)} %bitcast.43), channel_id=1, replica_groups=mesh['chip'=16,'core'=2,'tp'=8] {'chip'}, dimensions={0} | all-to-all | bytes 786432 | tf_op jit(solution)/shard_map/all_to_all | solution.py:488
  (80 shorter events, 33.2 us)
Async XLA Ops:
  2.3 15.3 %all-to-all-start = ((bf16[32,32,128]{2,1,0:T(8,128)(2,1)}), bf16[32,32,128]{2,1,0:T(8,128)(2,1)S(1)}, u32[]{:S(2)}, u32[]{:S(2)}) async-start(bf16[32,32,128]{2,1,0:T(8,128)(2,1)} %bitcast.4), calls=%async_computation | async-start | bytes 524288 | tf_op jit(solution)/shard_map/all_to_all | solution.py:355
  10.0 67.8 %collective-permute-start = (bf16[3072,384]{1,0:T(8,128)(2,1)}, bf16[3072,384]{1,0:T(8,128)(2,1)}, u32[]{:S(2)}, u32[]{:S(2)}) collective-permute-start(bf16[3072,384]{1,0:T(8,128)(2,1)} %bitcast.28), channel_id=1, source_target_pairs={{0,8},{8,0},{1,9},{9,1},{2,10},{10,2},{3,11},{11,3},{4,12},{12,4},... | collective-permute-start | bytes 7077896 | tf_op jit(solution)/shard_map/ppermute | solution.py:329
  10.2 67.6 %collective-permute-start.1 = (bf16[3072,384]{1,0:T(8,128)(2,1)}, bf16[3072,384]{1,0:T(8,128)(2,1)}, u32[]{:S(2)}, u32[]{:S(2)}) collective-permute-start(bf16[3072,384]{1,0:T(8,128)(2,1)} %bitcast.33), channel_id=1, source_target_pairs={{0,8},{8,0},{1,9},{9,1},{2,10},{10,2},{3,11},{11,3},{4,12},{12,4},... | collective-permute-start | bytes 7077896 | tf_op jit(solution)/shard_map/ppermute | solution.py:329
  10.5 67.2 %collective-permute-start.2 = (bf16[384,3072]{1,0:T(8,128)(2,1)}, bf16[384,3072]{1,0:T(8,128)(2,1)}, u32[]{:S(2)}, u32[]{:S(2)}) collective-permute-start(bf16[384,3072]{1,0:T(8,128)(2,1)} %bitcast.38), channel_id=1, source_target_pairs={{0,8},{8,0},{1,9},{9,1},{2,10},{10,2},{3,11},{11,3},{4,12},{12,4},... | collective-permute-start | bytes 7077896 | tf_op jit(solution)/shard_map/ppermute | solution.py:329
  18.4 11.7 %all-to-all-start.1 = ((bf16[32,16,128]{2,1,0:T(8,128)(2,1)}), bf16[32,16,128]{2,1,0:T(8,128)(2,1)S(1)}, u32[]{:S(2)}, u32[]{:S(2)}) async-start(bf16[32,16,128]{2,1,0:T(8,128)(2,1)} %get-tuple-element.122), calls=%async_computation.1 | async-start | bytes 262144 | tf_op jit(solution)/shard_map/all_to_all | solution.py:374
  77.8 9.0 %collective-permute-start.7 = (bf16[256,384]{1,0:T(8,128)(2,1)S(1)}, bf16[256,384]{1,0:T(8,128)(2,1)S(1)}, u32[]{:S(2)}, u32[]{:S(2)}) collective-permute-start(bf16[256,384]{1,0:T(8,128)(2,1)S(1)} %bitcast.20), channel_id=1, source_target_pairs={{0,1},{1,2},{2,3},{3,4},{4,5},{5,6},{6,7},{7,0},{8,9},{9,10},{10,1... | collective-permute-start | bytes 589832 | tf_op jit(solution)/shard_map/ppermute | solution.py:320
  81.1 12.2 %collective-permute-start.3 = (bf16[256,384]{1,0:T(8,128)(2,1)S(1)}, bf16[256,384]{1,0:T(8,128)(2,1)S(1)}, u32[]{:S(2)}, u32[]{:S(2)}) collective-permute-start(bf16[256,384]{1,0:T(8,128)(2,1)S(1)} %bitcast.23), channel_id=1, source_target_pairs={{0,1},{1,2},{2,3},{3,4},{4,5},{5,6},{6,7},{7,0},{8,9},{9,10},{10,1... | collective-permute-start | bytes 589832 | tf_op jit(solution)/shard_map/ppermute | solution.py:320
  81.1 12.2 %collective-permute-start.4 = (bf16[256,384]{1,0:T(8,128)(2,1)S(1)}, bf16[256,384]{1,0:T(8,128)(2,1)S(1)}, u32[]{:S(2)}, u32[]{:S(2)}) collective-permute-start(bf16[256,384]{1,0:T(8,128)(2,1)S(1)} %bitcast.24), channel_id=1, source_target_pairs={{0,7},{1,0},{2,1},{3,2},{4,3},{5,4},{6,5},{7,6},{8,15},{9,8},{10,9... | collective-permute-start | bytes 589832 | tf_op jit(solution)/shard_map/ppermute | solution.py:320
  86.8 9.9 %collective-permute-start.11 = (bf16[256,384]{1,0:T(8,128)(2,1)S(1)}, bf16[256,384]{1,0:T(8,128)(2,1)S(1)}, u32[]{:S(2)}, u32[]{:S(2)}) collective-permute-start(bf16[256,384]{1,0:T(8,128)(2,1)S(1)} %collective-permute-done.7.refs_8_), channel_id=1, source_target_pairs={{0,1},{1,2},{2,3},{3,4},{4,5},{5,6},{6,7},{7,0},{8,9},{9,10},{10,1... | collective-permute-start | bytes 589832 | tf_op jit(solution)/shard_map/ppermute | solution.py:320
  86.8 9.9 %collective-permute-start.12 = (bf16[256,384]{1,0:T(8,128)(2,1)S(1)}, bf16[256,384]{1,0:T(8,128)(2,1)S(1)}, u32[]{:S(2)}, u32[]{:S(2)}) collective-permute-start(bf16[256,384]{1,0:T(8,128)(2,1)S(1)} %collective-permute-done.8.refs_9_), channel_id=1, source_target_pairs={{0,7},{1,0},{2,1},{3,2},{4,3},{5,4},{6,5},{7,6},{8,15},{9,8},{10,9... | collective-permute-start | bytes 589832 | tf_op jit(solution)/shard_map/ppermute | solution.py:320
  93.4 11.1 %collective-permute-start.5 = (bf16[256,384]{1,0:T(8,128)(2,1)S(1)}, bf16[256,384]{1,0:T(8,128)(2,1)S(1)}, u32[]{:S(2)}, u32[]{:S(2)}) collective-permute-start(bf16[256,384]{1,0:T(8,128)(2,1)S(1)} %collective-permute-done.3.refs_6_), channel_id=1, source_target_pairs={{0,1},{1,2},{2,3},{3,4},{4,5},{5,6},{6,7},{7,0},{8,9},{9,10},{10,1... | collective-permute-start | bytes 589832 | tf_op jit(solution)/shard_map/ppermute | solution.py:320
  93.5 11.0 %collective-permute-start.6 = (bf16[256,384]{1,0:T(8,128)(2,1)S(1)}, bf16[256,384]{1,0:T(8,128)(2,1)S(1)}, u32[]{:S(2)}, u32[]{:S(2)}) collective-permute-start(bf16[256,384]{1,0:T(8,128)(2,1)S(1)} %collective-permute-done.4.refs_7_), channel_id=1, source_target_pairs={{0,7},{1,0},{2,1},{3,2},{4,3},{5,4},{6,5},{7,6},{8,15},{9,8},{10,9... | collective-permute-start | bytes 589832 | tf_op jit(solution)/shard_map/ppermute | solution.py:320
  96.7 11.1 %collective-permute-start.13 = (bf16[256,384]{1,0:T(8,128)(2,1)S(1)}, bf16[256,384]{1,0:T(8,128)(2,1)S(1)}, u32[]{:S(2)}, u32[]{:S(2)}) collective-permute-start(bf16[256,384]{1,0:T(8,128)(2,1)S(1)} %collective-permute-done.11.refs_8_), channel_id=1, source_target_pairs={{0,1},{1,2},{2,3},{3,4},{4,5},{5,6},{6,7},{7,0},{8,9},{9,10},{10,1... | collective-permute-start | bytes 589832 | tf_op jit(solution)/shard_map/ppermute | solution.py:320
  96.7 11.1 %collective-permute-start.14 = (bf16[256,384]{1,0:T(8,128)(2,1)S(1)}, bf16[256,384]{1,0:T(8,128)(2,1)S(1)}, u32[]{:S(2)}, u32[]{:S(2)}) collective-permute-start(bf16[256,384]{1,0:T(8,128)(2,1)S(1)} %collective-permute-done.12.refs_9_), channel_id=1, source_target_pairs={{0,7},{1,0},{2,1},{3,2},{4,3},{5,4},{6,5},{7,6},{8,15},{9,8},{10,9... | collective-permute-start | bytes 589832 | tf_op jit(solution)/shard_map/ppermute | solution.py:320
  104.5 8.7 %collective-permute-start.9 = (bf16[256,384]{1,0:T(8,128)(2,1)S(1)}, bf16[256,384]{1,0:T(8,128)(2,1)S(1)}, u32[]{:S(2)}, u32[]{:S(2)}) collective-permute-start(bf16[256,384]{1,0:T(8,128)(2,1)S(1)} %collective-permute-done.5.refs_6_), channel_id=1, source_target_pairs={{0,1},{1,2},{2,3},{3,4},{4,5},{5,6},{6,7},{7,0},{8,9},{9,10},{10,1... | collective-permute-start | bytes 589832 | tf_op jit(solution)/shard_map/ppermute | solution.py:320
  107.8 9.3 %collective-permute-start.16 = (bf16[256,384]{1,0:T(8,128)(2,1)S(1)}, bf16[256,384]{1,0:T(8,128)(2,1)S(1)}, u32[]{:S(2)}, u32[]{:S(2)}) collective-permute-start(bf16[256,384]{1,0:T(8,128)(2,1)S(1)} %collective-permute-done.14.refs_9_), channel_id=1, source_target_pairs={{0,7},{1,0},{2,1},{3,2},{4,3},{5,4},{6,5},{7,6},{8,15},{9,8},{10,9... | collective-permute-start | bytes 589832 | tf_op jit(solution)/shard_map/ppermute | solution.py:320
  113.2 9.6 %collective-permute-start.15 = (bf16[256,384]{1,0:T(8,128)(2,1)S(1)}, bf16[256,384]{1,0:T(8,128)(2,1)S(1)}, u32[]{:S(2)}, u32[]{:S(2)}) collective-permute-start(bf16[256,384]{1,0:T(8,128)(2,1)S(1)} %collective-permute-done.9.refs_0_), channel_id=1, source_target_pairs={{0,1},{1,2},{2,3},{3,4},{4,5},{5,6},{6,7},{7,0},{8,9},{9,10},{10,1... | collective-permute-start | bytes 589832 | tf_op jit(solution)/shard_map/ppermute | solution.py:320
  119.5 10.8 %collective-permute-start.24 = (bf16[256,384]{1,0:T(8,128)(2,1)S(1)}, bf16[256,384]{1,0:T(8,128)(2,1)S(1)}, u32[]{:S(2)}, u32[]{:S(2)}) collective-permute-start(bf16[256,384]{1,0:T(8,128)(2,1)S(1)} %get-tuple-element.211), channel_id=1, source_target_pairs={{0,1},{1,2},{2,3},{3,4},{4,5},{5,6},{6,7},{7,0},{8,9},{9,10},{10,1... | collective-permute-start | bytes 589832 | tf_op jit(solution)/shard_map/ppermute | solution.py:320
  119.6 10.7 %collective-permute-start.25 = (bf16[256,384]{1,0:T(8,128)(2,1)S(1)}, bf16[256,384]{1,0:T(8,128)(2,1)S(1)}, u32[]{:S(2)}, u32[]{:S(2)}) collective-permute-start(bf16[256,384]{1,0:T(8,128)(2,1)S(1)} %get-tuple-element.212), channel_id=1, source_target_pairs={{0,7},{1,0},{2,1},{3,2},{4,3},{5,4},{6,5},{7,6},{8,15},{9,8},{10,9... | collective-permute-start | bytes 589832 | tf_op jit(solution)/shard_map/ppermute | solution.py:320
  130.4 8.8 %collective-permute-start.26 = (bf16[256,384]{1,0:T(8,128)(2,1)S(1)}, bf16[256,384]{1,0:T(8,128)(2,1)S(1)}, u32[]{:S(2)}, u32[]{:S(2)}) collective-permute-start(bf16[256,384]{1,0:T(8,128)(2,1)S(1)} %add_convert_fusion.5), channel_id=1, source_target_pairs={{0,1},{1,2},{2,3},{3,4},{4,5},{5,6},{6,7},{7,0},{8,9},{9,10},{10,1... | collective-permute-start | bytes 589832 | tf_op jit(solution)/shard_map/ppermute | solution.py:320
  133.9 9.1 %collective-permute-start.19 = (bf16[256,384]{1,0:T(8,128)(2,1)S(1)}, bf16[256,384]{1,0:T(8,128)(2,1)S(1)}, u32[]{:S(2)}, u32[]{:S(2)}) collective-permute-start(bf16[256,384]{1,0:T(8,128)(2,1)S(1)} %add_convert_fusion.11), channel_id=1, source_target_pairs={{0,1},{1,2},{2,3},{3,4},{4,5},{5,6},{6,7},{7,0},{8,9},{9,10},{10,1... | collective-permute-start | bytes 589832 | tf_op jit(solution)/shard_map/ppermute | solution.py:320
  134.0 9.2 %collective-permute-start.20 = (bf16[256,384]{1,0:T(8,128)(2,1)S(1)}, bf16[256,384]{1,0:T(8,128)(2,1)S(1)}, u32[]{:S(2)}, u32[]{:S(2)}) collective-permute-start(bf16[256,384]{1,0:T(8,128)(2,1)S(1)} %add_convert_fusion.10), channel_id=1, source_target_pairs={{0,7},{1,0},{2,1},{3,2},{4,3},{5,4},{6,5},{7,6},{8,15},{9,8},{10,9... | collective-permute-start | bytes 589832 | tf_op jit(solution)/shard_map/ppermute | solution.py:320
  139.2 9.0 %collective-permute-start.28 = (bf16[256,384]{1,0:T(8,128)(2,1)S(1)}, bf16[256,384]{1,0:T(8,128)(2,1)S(1)}, u32[]{:S(2)}, u32[]{:S(2)}) collective-permute-start(bf16[256,384]{1,0:T(8,128)(2,1)S(1)} %add_convert_fusion.3), channel_id=1, source_target_pairs={{0,1},{1,2},{2,3},{3,4},{4,5},{5,6},{6,7},{7,0},{8,9},{9,10},{10,1... | collective-permute-start | bytes 589832 | tf_op jit(solution)/shard_map/ppermute | solution.py:320
  139.4 8.8 %collective-permute-start.29 = (bf16[256,384]{1,0:T(8,128)(2,1)S(1)}, bf16[256,384]{1,0:T(8,128)(2,1)S(1)}, u32[]{:S(2)}, u32[]{:S(2)}) collective-permute-start(bf16[256,384]{1,0:T(8,128)(2,1)S(1)} %add_convert_fusion.2), channel_id=1, source_target_pairs={{0,7},{1,0},{2,1},{3,2},{4,3},{5,4},{6,5},{7,6},{8,15},{9,8},{10,9... | collective-permute-start | bytes 589832 | tf_op jit(solution)/shard_map/ppermute | solution.py:320
  (11 other events, 74.5 us)

commit v2 on v1

--- a/solution.py
+++ b/solution.py
@@ -202,8 +202,9 @@
         copy.wait()
 
 
-def first_load_kernel(place, gain, router, others, *refs, rows, columns):
-    weights, downs, (gate_up, down, inverse, router_out, others_out, *sems) = refs[:4], refs[4:6], refs[6:]
+def first_load_kernel(place, gain, router, others, *refs, rows, columns, capacity):
+    weights, downs, (gate_up, down, inverse, router_out, *other, row_sems, column_sems) = refs[:4], refs[4:6], refs[6:]
+    sems = row_sems, column_sems
     peers = gain.shape[0]
     copies = row_copies(place, weights, gate_up, sems[0], rows, peers)
     copies += column_copies(place, downs, down, sems[1], columns, peers)
@@ -211,13 +212,14 @@
         copy.start()
     inverse[...] = 1.0 / gain[...]
     router_out[...] = router[...]
-    others_out[...] = others[...]
+    for h in range(2):
+        found = other_experts(place, others, other[h].shape[0], h, capacity)
+        other[h][...] = jnp.broadcast_to(found, other[h].shape)
     for copy in copies:
         copy.wait()
 
 
-def mixing_of(place, others, logits, h, capacity):
-    rows, experts = logits.shape
+def other_experts(place, others, rows, h, capacity):
     blocks, lanes = others.shape
     row = lax.broadcasted_iota(jnp.int32, (rows, blocks), 0)
     block = lax.broadcasted_iota(jnp.int32, (rows, blocks), 1)
@@ -226,9 +228,12 @@
     row = lax.broadcasted_iota(jnp.int32, (rows, lanes), 0)
     lane = lax.broadcasted_iota(jnp.int32, (rows, lanes), 1)
     own_lane = lax.rem(place[2], lanes // capacity) * capacity + lax.rem(row, capacity)
-    other = jnp.sum(jnp.where(lane == own_lane, from_sender, 0.0), axis=1, keepdims=True).astype(jnp.int32)
-    expert = lax.broadcasted_iota(jnp.int32, (rows, experts), 1)
-    sign = (expert == place[2]).astype(f32) - (expert == other).astype(f32)
+    return jnp.sum(jnp.where(lane == own_lane, from_sender, 0.0), axis=1, keepdims=True)
+
+
+def mixing_of(place, other, logits):
+    expert = lax.broadcasted_iota(jnp.int32, logits.shape, 1)
+    sign = (expert == place[2]).astype(f32) - (expert == other.astype(jnp.int32)).astype(f32)
     return jax.nn.sigmoid(jnp.sum(sign * logits, axis=1, keepdims=True))
 
 
@@ -242,7 +247,7 @@
 
 
 def far_products_kernel(
-    place, inverse, router, gate_up, down, others, total, beside, *refs, order, h, far, width, capacity
+    place, inverse, router, gate_up, down, other, total, beside, *refs, order, far, width
 ):
     count = len(order)
     outs, activated = refs[count:-1], refs[-1]
@@ -251,7 +256,7 @@
     sums += beside[...]
     experts = router.shape[0]
     scale = lax.rsqrt(sums[:, experts:experts + 1] / width + epsilon)
-    mixing = mixing_of(place, others, sums[:, :experts] * scale, h, capacity)
+    mixing = mixing_of(place, other[:, 0:1], sums[:, :experts] * scale)
     both = (total[...] + product) * scale
     gated = both[:, :units]
     active = (gated * jax.nn.sigmoid(gated) * both[:, units:] * mixing).astype(bf16)
@@ -261,9 +266,11 @@
 
 
 def near_products_kernel(active_a, active_b, down, *outs, near):
-    for h, active in enumerate((active_a, active_b)):
-        for k, piece in enumerate(products(active[...], down, 0, near, outs[0].shape[1])):
-            outs[2 * k + h][...] = piece
+    half, width = outs[0].shape
+    active = jnp.concatenate([active_a[...], active_b[...]], axis=0)
+    for k, piece in enumerate(products(active, down, 0, near, width)):
+        outs[2 * k][...] = piece[:half]
+        outs[2 * k + 1][...] = piece[half:]
 
 
 def combine_kernel(returned, hidden, chosen, out):
@@ -431,9 +438,9 @@
             loaded = kept(
                 first_load_kernel,
                 (wide, pltpu.VMEM((units, len(far) * share), bf16), pltpu.VMEM(gain.shape, f32),
-                 pltpu.VMEM(router.shape, bf16), pltpu.VMEM(others.shape, f32)),
+                 pltpu.VMEM(router.shape, bf16)) + (pltpu.VMEM((half, 128), f32),) * 2,
                 0, [smem] + [vmem] * 3 + [hbm] * 6, [place, gain, router, others, *sides, *downs], semaphores,
-                rows=parts[0], columns=far,
+                rows=parts[0], columns=far, capacity=capacity,
             )
         elif distance == 2:
             *totals, gate_up, down_near = loaded = kept(
@@ -450,7 +457,7 @@
         moving[0], loaded = tied((moving[0], loaded))
         if distance == 1:
             gate_up, down_far, *small = loaded
-            inverse, router, others = [in_vmem(x) for x in small]
+            inverse, router, *other_halves = [in_vmem(x) for x in small]
         elif distance == 2:
             *totals, gate_up, down_near = loaded
         else:
@@ -468,8 +475,8 @@
     ready = [
         kept(
             far_products_kernel, (piece,) * len(far) + (struct((half, units), bf16),), work, [smem],
-            [place, inverse, router, gate_up_last, down_far, others, *totals[2 * h:2 * h + 2], *[got[h][k] for k in parts[3]]],
-            order=parts[3], h=h, far=len(far), width=width, capacity=capacity,
+            [place, inverse, router, gate_up_last, down_far, other_halves[h], *totals[2 * h:2 * h + 2], *[got[h][k] for k in parts[3]]],
+            order=parts[3], far=len(far), width=width,
         )
         for h in range(2)
     ]

time: 172 us -> 171 us (level)
  transfers between devices with their start and end apart: 33 -> 33, of which waited for: 10 -> 10; matrix products, arithmetic and copies ran while one was open for 0% -> 0% of each run, Pallas kernels for 18% -> 17%
where the time goes in v2:
time: 171 us
  blocking collectives  57.6 us (34%)
  starting transfers between devices  57.5 us (34%)
  Pallas kernels  32.9 us (19%)
  waiting for transfers between devices  21.4 us (13%)
    ppermute x28, starting transfers between devices, moved(): lax.ppermute(piece, 'tp', [(i, (i + step) % peers) for i in range(peers)])  44.2 us
    all_to_all x1, blocking collectives, shards(): partial = lax.all_to_all(partial, 'tp', 0, 0, tiled=True)  31.7 us
    pallas_call x7, Pallas kernels, kept(): pl.pallas_call(functools.partial(kernel, **options), out_shape=shapes, in...  20.9 us
    all_to_all x1, blocking collectives, shards(): lax.all_to_all(outgoing.reshape(chips, capacity, share), 'chip', 0, 0, ti...  13.6 us
    ppermute x28, waiting for transfers between devices, moved(): lax.ppermute(piece, 'tp', [(i, (i + step) % peers) for i in range(peers)])  13.6 us
    all_to_all x1, blocking collectives, shards(): lax.all_to_all(summed.reshape(chips, capacity, share), 'chip', 0, 0, tile...  12.3 us
    pallas_call x5, Pallas kernels, call(): pl.pallas_call(kernel, out_shape=shapes, compiler_params=pltpu.CompilerPa...  7.8 us
    all_to_all x1, starting transfers between devices, shards(): lax.all_to_all(parts.reshape(blocks, 2 * rows, size), ('chip', 'core'), 0...  7.62 us
  transfers between devices with their start and end apart: 33, of which 10 were waited for; matrix products, arithmetic and copies ran while one was open for 0% of the time, Pallas kernels for 17%

profile of v2, /device:TPU:2, one launch (start us, length us, event | category | flops | bytes accessed | tf_op | source)
XLA Modules:
  0.0 170.6 jit_solution(5309706512852932691)
XLA Ops:
  2.3 7.6 %all-to-all-start = ((bf16[32,32,128]{2,1,0:T(8,128)(2,1)}), bf16[32,32,128]{2,1,0:T(8,128)(2,1)S(1)}, u32[]{:S(2)}, u32[]{:S(2)}) async-start(bf16[32,32,128]{2,1,0:T(8,128)(2,1)} %bitcast.4), calls=%async_computation | async-start | bytes 524288 | tf_op jit(solution)/shard_map/all_to_all | solution.py:362
  11.4 6.2 %all-to-all-done.received = bf16[32,32,128]{2,1,0:T(8,128)(2,1)S(1)} async-done(((bf16[32,32,128]{2,1,0:T(8,128)(2,1)}), bf16[32,32,128]{2,1,0:T(8,128)(2,1)S(1)}, u32[]{:S(2)}, u32[]{:S(2)}) %all-to-all-start) | async-done | bytes 262176 | tf_op jit(solution)/shard_map/all_to_all | solution.py:362
  18.4 5.0 %all-to-all-start.1 = ((bf16[32,16,128]{2,1,0:T(8,128)(2,1)}), bf16[32,16,128]{2,1,0:T(8,128)(2,1)S(1)}, u32[]{:S(2)}, u32[]{:S(2)}) async-start(bf16[32,16,128]{2,1,0:T(8,128)(2,1)} %get-tuple-element.124), calls=%async_computation.1 | async-start | bytes 262144 | tf_op jit(solution)/shard_map/all_to_all | solution.py:381
  32.0 31.7 %all_to_all.25.partial = bf16[8,128,384]{2,1,0:T(8,128)(2,1)S(1)} all-to-all(bf16[8,128,384]{2,1,0:T(8,128)(2,1)S(1)} %shard_map.150), channel_id=1, replica_groups=mesh['chip'=16,'core'=2,'tp'=8] {'tp'}, dimensions={0} | all-to-all | bytes 1572864 | tf_op jit(solution)/shard_map/all_to_all | solution.py:389
  64.1 13.6 %all_to_all.26 = bf16[16,32,384]{2,1,0:T(8,128)(2,1)S(1)} all-to-all(bf16[16,32,384]{2,1,0:T(8,128)(2,1)S(1)} %bitcast.27), channel_id=1, replica_groups=mesh['chip'=16,'core'=2,'tp'=8] {'chip'}, dimensions={0} | all-to-all | bytes 786432 | tf_op jit(solution)/shard_map/all_to_all | solution.py:399
  78.4 2.7 %collective-permute-start.8 = (bf16[256,384]{1,0:T(8,128)(2,1)S(1)}, bf16[256,384]{1,0:T(8,128)(2,1)S(1)}, u32[]{:S(2)}, u32[]{:S(2)}) collective-permute-start(bf16[256,384]{1,0:T(8,128)(2,1)S(1)} %bitcast.21), channel_id=1, source_target_pairs={{0,7},{1,0},{2,1},{3,2},{4,3},{5,4},{6,5},{7,6},{8,15},{9,8},{10,9... | collective-permute-start | bytes 589832 | tf_op jit(solution)/shard_map/ppermute | solution.py:327
  81.1 3.2 %collective-permute-start.4 = (bf16[256,384]{1,0:T(8,128)(2,1)S(1)}, bf16[256,384]{1,0:T(8,128)(2,1)S(1)}, u32[]{:S(2)}, u32[]{:S(2)}) collective-permute-start(bf16[256,384]{1,0:T(8,128)(2,1)S(1)} %bitcast.24), channel_id=1, source_target_pairs={{0,7},{1,0},{2,1},{3,2},{4,3},{5,4},{6,5},{7,6},{8,15},{9,8},{10,9... | collective-permute-start | bytes 589832 | tf_op jit(solution)/shard_map/ppermute | solution.py:327
  86.8 3.3 %collective-permute-start.12 = (bf16[256,384]{1,0:T(8,128)(2,1)S(1)}, bf16[256,384]{1,0:T(8,128)(2,1)S(1)}, u32[]{:S(2)}, u32[]{:S(2)}) collective-permute-start(bf16[256,384]{1,0:T(8,128)(2,1)S(1)} %collective-permute-done.8.refs_9_), channel_id=1, source_target_pairs={{0,7},{1,0},{2,1},{3,2},{4,3},{5,4},{6,5},{7,6},{8,15},{9,8},{10,9... | collective-permute-start | bytes 589832 | tf_op jit(solution)/shard_map/ppermute | solution.py:327
  90.1 3.3 %shard_map.153 = (bf16[768,1536]{1,0:T(8,128)(2,1)S(1)}, bf16[768,1152]{1,0:T(8,128)(2,1)S(1)}, f32[8,1,384]{2,1,0:T(1,128)S(1)}, bf16[16,3072]{1,0:T(8,128)(2,1...) custom-call(s32[3]{0:T(128)S(1)} %pad_add_fusion.place, f32[8,1,384]{2,1,0:T(1,128)} %bitcast.47, ...), custom_call_target="tpu_custom_call" | custom-call | bytes 4194304 | tf_op jit(solution)/shard_map/pallas_call | solution.py:420
  93.5 3.2 %collective-permute-start.6 = (bf16[256,384]{1,0:T(8,128)(2,1)S(1)}, bf16[256,384]{1,0:T(8,128)(2,1)S(1)}, u32[]{:S(2)}, u32[]{:S(2)}) collective-permute-start(bf16[256,384]{1,0:T(8,128)(2,1)S(1)} %collective-permute-done.4.refs_7_), channel_id=1, source_target_pairs={{0,7},{1,0},{2,1},{3,2},{4,3},{5,4},{6,5},{7,6},{8,15},{9,8},{10,9... | collective-permute-start | bytes 589832 | tf_op jit(solution)/shard_map/ppermute | solution.py:327
  96.8 3.2 %collective-permute-start.14 = (bf16[256,384]{1,0:T(8,128)(2,1)S(1)}, bf16[256,384]{1,0:T(8,128)(2,1)S(1)}, u32[]{:S(2)}, u32[]{:S(2)}) collective-permute-start(bf16[256,384]{1,0:T(8,128)(2,1)S(1)} %collective-permute-done.12.refs_9_), channel_id=1, source_target_pairs={{0,7},{1,0},{2,1},{3,2},{4,3},{5,4},{6,5},{7,6},{8,15},{9,8},{10,9... | collective-permute-start | bytes 589832 | tf_op jit(solution)/shard_map/ppermute | solution.py:327
  100.0 4.5 %shard_map.154 = (f32[256,1536]{1,0:T(8,128)S(1)}, f32[256,128]{1,0:T(8,128)S(1)}, f32[256,1536]{1,0:T(8,128)S(1)}, f32[256,128]{1,0:T(8,128)S(1)}, bf16[768,153...) custom-call(s32[3]{0:T(128)S(1)} %pad_add_fusion.place, f32[8,1,384]{2,1,0:T(1,128)S(1)} %get-tuple-element.146.inverse, ...), custom_call_target="tpu_custom_call" | custom-call | flops 1207959552 | bytes 4194304 | tf_op jit(solution)/shard_map/pallas_call | solution.py:420
  104.6 3.2 %collective-permute-start.10 = (bf16[256,384]{1,0:T(8,128)(2,1)S(1)}, bf16[256,384]{1,0:T(8,128)(2,1)S(1)}, u32[]{:S(2)}, u32[]{:S(2)}) collective-permute-start(bf16[256,384]{1,0:T(8,128)(2,1)S(1)} %collective-permute-done.6.refs_7_), channel_id=1, source_target_pairs={{0,7},{1,0},{2,1},{3,2},{4,3},{5,4},{6,5},{7,6},{8,15},{9,8},{10,9... | collective-permute-start | bytes 589832 | tf_op jit(solution)/shard_map/ppermute | solution.py:327
  108.9 3.6 %shard_map.155 = (f32[256,1536]{1,0:T(8,128)S(1)}, f32[256,128]{1,0:T(8,128)S(1)}, f32[256,1536]{1,0:T(8,128)S(1)}, f32[256,128]{1,0:T(8,128)S(1)}, bf16[768,1536]{1,0:T(8,128)(2,1)S(1)}) custom-call(s32[3]{0:T(128)S(1)} %pad_add_fusion.place, f32[8,1,384]{2,1,0:T(1,128)S(1)} %get-tuple-element.146.inverse, bf16[16,3072]{1,0:T(8,128)(2,1)S(1)} %get-tuple-element.147.router, ...), custom_call_target="tpu_custom_call" | custom-call | flops 1207959552 | bytes 4194304 | tf_op jit(solution)/shard_map/pallas_call | solution.py:420
  113.6 3.6 %shard_map.156 = (f32[256,1536]{1,0:T(8,128)S(1)}, f32[256,128]{1,0:T(8,128)S(1)}, f32[256,1536]{1,0:T(8,128)S(1)}, f32[256,128]{1,0:T(8,128)S(1)}, bf16[768,1536]{1,0:T(8,128)(2,1)S(1)}) custom-call(s32[3]{0:T(128)S(1)} %pad_add_fusion.place, f32[8,1,384]{2,1,0:T(1,128)S(1)} %get-tuple-element.146.inverse, bf16[16,3072]{1,0:T(8,128)(2,1)S(1)} %get-tuple-element.147.router, ...), custom_call_target="tpu_custom_call" | custom-call | flops 1207959552 | bytes 4194304 | tf_op jit(solution)/shard_map/pallas_call | solution.py:420
  119.3 3.2 %collective-permute-start.25 = (bf16[256,384]{1,0:T(8,128)(2,1)S(1)}, bf16[256,384]{1,0:T(8,128)(2,1)S(1)}, u32[]{:S(2)}, u32[]{:S(2)}) collective-permute-start(bf16[256,384]{1,0:T(8,128)(2,1)S(1)} %get-tuple-element.216), channel_id=1, source_target_pairs={{0,7},{1,0},{2,1},{3,2},{4,3},{5,4},{6,5},{7,6},{8,15},{9,8},{10,9... | collective-permute-start | bytes 589832 | tf_op jit(solution)/shard_map/ppermute | solution.py:327
  124.9 3.2 %collective-permute-start.18 = (bf16[256,384]{1,0:T(8,128)(2,1)S(1)}, bf16[256,384]{1,0:T(8,128)(2,1)S(1)}, u32[]{:S(2)}, u32[]{:S(2)}) collective-permute-start(bf16[256,384]{1,0:T(8,128)(2,1)S(1)} %get-tuple-element.202), channel_id=1, source_target_pairs={{0,7},{1,0},{2,1},{3,2},{4,3},{5,4},{6,5},{7,6},{8,15},{9,8},{10,9... | collective-permute-start | bytes 589832 | tf_op jit(solution)/shard_map/ppermute | solution.py:327
  130.2 3.3 %collective-permute-start.27 = (bf16[256,384]{1,0:T(8,128)(2,1)S(1)}, bf16[256,384]{1,0:T(8,128)(2,1)S(1)}, u32[]{:S(2)}, u32[]{:S(2)}) collective-permute-start(bf16[256,384]{1,0:T(8,128)(2,1)S(1)} %add_convert_fusion.4), channel_id=1, source_target_pairs={{0,7},{1,0},{2,1},{3,2},{4,3},{5,4},{6,5},{7,6},{8,15},{9,8},{10,9... | collective-permute-start | bytes 589832 | tf_op jit(solution)/shard_map/ppermute | solution.py:327
  133.7 3.3 %collective-permute-start.20 = (bf16[256,384]{1,0:T(8,128)(2,1)S(1)}, bf16[256,384]{1,0:T(8,128)(2,1)S(1)}, u32[]{:S(2)}, u32[]{:S(2)}) collective-permute-start(bf16[256,384]{1,0:T(8,128)(2,1)S(1)} %add_convert_fusion.10), channel_id=1, source_target_pairs={{0,7},{1,0},{2,1},{3,2},{4,3},{5,4},{6,5},{7,6},{8,15},{9,8},{10,9... | collective-permute-start | bytes 589832 | tf_op jit(solution)/shard_map/ppermute | solution.py:327
  138.8 3.6 %collective-permute-start.29 = (bf16[256,384]{1,0:T(8,128)(2,1)S(1)}, bf16[256,384]{1,0:T(8,128)(2,1)S(1)}, u32[]{:S(2)}, u32[]{:S(2)}) collective-permute-start(bf16[256,384]{1,0:T(8,128)(2,1)S(1)} %add_convert_fusion.2), channel_id=1, source_target_pairs={{0,7},{1,0},{2,1},{3,2},{4,3},{5,4},{6,5},{7,6},{8,15},{9,8},{10,9... | collective-permute-start | bytes 589832 | tf_op jit(solution)/shard_map/ppermute | solution.py:327
  142.9 3.8 %collective-permute-start.22 = (bf16[256,384]{1,0:T(8,128)(2,1)S(1)}, bf16[256,384]{1,0:T(8,128)(2,1)S(1)}, u32[]{:S(2)}, u32[]{:S(2)}) collective-permute-start(bf16[256,384]{1,0:T(8,128)(2,1)S(1)} %add_convert_fusion.8), channel_id=1, source_target_pairs={{0,7},{1,0},{2,1},{3,2},{4,3},{5,4},{6,5},{7,6},{8,15},{9,8},{10,9... | collective-permute-start | bytes 589832 | tf_op jit(solution)/shard_map/ppermute | solution.py:327
  150.4 3.5 %collective-permute-done.30 = bf16[256,384]{1,0:T(8,128)(2,1)S(1)} collective-permute-done((bf16[256,384]{1,0:T(8,128)(2,1)S(1)}, bf16[256,384]{1,0:T(8,128)(2,1)S(1)}, u32[]{:S(2)}, u32[]{:S(2)}) %collective-permute-start.30) | collective-permute-done | bytes 196640 | tf_op jit(solution)/shard_map/ppermute | solution.py:327
  153.9 3.4 %collective-permute-done.23 = bf16[256,384]{1,0:T(8,128)(2,1)S(1)} collective-permute-done((bf16[256,384]{1,0:T(8,128)(2,1)S(1)}, bf16[256,384]{1,0:T(8,128)(2,1)S(1)}, u32[]{:S(2)}, u32[]{:S(2)}) %collective-permute-start.23) | collective-permute-done | bytes 196640 | tf_op jit(solution)/shard_map/ppermute | solution.py:327
  157.5 12.3 %all_to_all.27 = bf16[16,32,384]{2,1,0:T(8,128)(2,1)S(1)} all-to-all(bf16[16,32,384]{2,1,0:T(8,128)(2,1)S(1)} %bitcast.43), channel_id=1, replica_groups=mesh['chip'=16,'core'=2,'tp'=8] {'chip'}, dimensions={0} | all-to-all | bytes 786432 | tf_op jit(solution)/shard_map/all_to_all | solution.py:495
  (80 shorter events, 32.6 us)
Async XLA Ops:
  2.3 15.3 %all-to-all-start = ((bf16[32,32,128]{2,1,0:T(8,128)(2,1)}), bf16[32,32,128]{2,1,0:T(8,128)(2,1)S(1)}, u32[]{:S(2)}, u32[]{:S(2)}) async-start(bf16[32,32,128]{2,1,0:T(8,128)(2,1)} %bitcast.4), calls=%async_computation | async-start | bytes 524288 | tf_op jit(solution)/shard_map/all_to_all | solution.py:362
  10.0 67.8 %collective-permute-start = (bf16[3072,384]{1,0:T(8,128)(2,1)}, bf16[3072,384]{1,0:T(8,128)(2,1)}, u32[]{:S(2)}, u32[]{:S(2)}) collective-permute-start(bf16[3072,384]{1,0:T(8,128)(2,1)} %bitcast.28), channel_id=1, source_target_pairs={{0,8},{8,0},{1,9},{9,1},{2,10},{10,2},{3,11},{11,3},{4,12},{12,4},... | collective-permute-start | bytes 7077896 | tf_op jit(solution)/shard_map/ppermute | solution.py:336
  10.2 67.6 %collective-permute-start.1 = (bf16[3072,384]{1,0:T(8,128)(2,1)}, bf16[3072,384]{1,0:T(8,128)(2,1)}, u32[]{:S(2)}, u32[]{:S(2)}) collective-permute-start(bf16[3072,384]{1,0:T(8,128)(2,1)} %bitcast.33), channel_id=1, source_target_pairs={{0,8},{8,0},{1,9},{9,1},{2,10},{10,2},{3,11},{11,3},{4,12},{12,4},... | collective-permute-start | bytes 7077896 | tf_op jit(solution)/shard_map/ppermute | solution.py:336
  10.5 67.2 %collective-permute-start.2 = (bf16[384,3072]{1,0:T(8,128)(2,1)}, bf16[384,3072]{1,0:T(8,128)(2,1)}, u32[]{:S(2)}, u32[]{:S(2)}) collective-permute-start(bf16[384,3072]{1,0:T(8,128)(2,1)} %bitcast.38), channel_id=1, source_target_pairs={{0,8},{8,0},{1,9},{9,1},{2,10},{10,2},{3,11},{11,3},{4,12},{12,4},... | collective-permute-start | bytes 7077896 | tf_op jit(solution)/shard_map/ppermute | solution.py:336
  18.4 11.7 %all-to-all-start.1 = ((bf16[32,16,128]{2,1,0:T(8,128)(2,1)}), bf16[32,16,128]{2,1,0:T(8,128)(2,1)S(1)}, u32[]{:S(2)}, u32[]{:S(2)}) async-start(bf16[32,16,128]{2,1,0:T(8,128)(2,1)} %get-tuple-element.124), calls=%async_computation.1 | async-start | bytes 262144 | tf_op jit(solution)/shard_map/all_to_all | solution.py:381
  77.8 9.0 %collective-permute-start.7 = (bf16[256,384]{1,0:T(8,128)(2,1)S(1)}, bf16[256,384]{1,0:T(8,128)(2,1)S(1)}, u32[]{:S(2)}, u32[]{:S(2)}) collective-permute-start(bf16[256,384]{1,0:T(8,128)(2,1)S(1)} %bitcast.20), channel_id=1, source_target_pairs={{0,1},{1,2},{2,3},{3,4},{4,5},{5,6},{6,7},{7,0},{8,9},{9,10},{10,1... | collective-permute-start | bytes 589832 | tf_op jit(solution)/shard_map/ppermute | solution.py:327
  81.1 12.3 %collective-permute-start.3 = (bf16[256,384]{1,0:T(8,128)(2,1)S(1)}, bf16[256,384]{1,0:T(8,128)(2,1)S(1)}, u32[]{:S(2)}, u32[]{:S(2)}) collective-permute-start(bf16[256,384]{1,0:T(8,128)(2,1)S(1)} %bitcast.23), channel_id=1, source_target_pairs={{0,1},{1,2},{2,3},{3,4},{4,5},{5,6},{6,7},{7,0},{8,9},{9,10},{10,1... | collective-permute-start | bytes 589832 | tf_op jit(solution)/shard_map/ppermute | solution.py:327
  81.1 12.3 %collective-permute-start.4 = (bf16[256,384]{1,0:T(8,128)(2,1)S(1)}, bf16[256,384]{1,0:T(8,128)(2,1)S(1)}, u32[]{:S(2)}, u32[]{:S(2)}) collective-permute-start(bf16[256,384]{1,0:T(8,128)(2,1)S(1)} %bitcast.24), channel_id=1, source_target_pairs={{0,7},{1,0},{2,1},{3,2},{4,3},{5,4},{6,5},{7,6},{8,15},{9,8},{10,9... | collective-permute-start | bytes 589832 | tf_op jit(solution)/shard_map/ppermute | solution.py:327
  86.8 9.9 %collective-permute-start.11 = (bf16[256,384]{1,0:T(8,128)(2,1)S(1)}, bf16[256,384]{1,0:T(8,128)(2,1)S(1)}, u32[]{:S(2)}, u32[]{:S(2)}) collective-permute-start(bf16[256,384]{1,0:T(8,128)(2,1)S(1)} %collective-permute-done.7.refs_8_), channel_id=1, source_target_pairs={{0,1},{1,2},{2,3},{3,4},{4,5},{5,6},{6,7},{7,0},{8,9},{9,10},{10,1... | collective-permute-start | bytes 589832 | tf_op jit(solution)/shard_map/ppermute | solution.py:327
  86.8 9.9 %collective-permute-start.12 = (bf16[256,384]{1,0:T(8,128)(2,1)S(1)}, bf16[256,384]{1,0:T(8,128)(2,1)S(1)}, u32[]{:S(2)}, u32[]{:S(2)}) collective-permute-start(bf16[256,384]{1,0:T(8,128)(2,1)S(1)} %collective-permute-done.8.refs_9_), channel_id=1, source_target_pairs={{0,7},{1,0},{2,1},{3,2},{4,3},{5,4},{6,5},{7,6},{8,15},{9,8},{10,9... | collective-permute-start | bytes 589832 | tf_op jit(solution)/shard_map/ppermute | solution.py:327
  93.4 11.1 %collective-permute-start.5 = (bf16[256,384]{1,0:T(8,128)(2,1)S(1)}, bf16[256,384]{1,0:T(8,128)(2,1)S(1)}, u32[]{:S(2)}, u32[]{:S(2)}) collective-permute-start(bf16[256,384]{1,0:T(8,128)(2,1)S(1)} %collective-permute-done.3.refs_6_), channel_id=1, source_target_pairs={{0,1},{1,2},{2,3},{3,4},{4,5},{5,6},{6,7},{7,0},{8,9},{9,10},{10,1... | collective-permute-start | bytes 589832 | tf_op jit(solution)/shard_map/ppermute | solution.py:327
  93.5 11.0 %collective-permute-start.6 = (bf16[256,384]{1,0:T(8,128)(2,1)S(1)}, bf16[256,384]{1,0:T(8,128)(2,1)S(1)}, u32[]{:S(2)}, u32[]{:S(2)}) collective-permute-start(bf16[256,384]{1,0:T(8,128)(2,1)S(1)} %collective-permute-done.4.refs_7_), channel_id=1, source_target_pairs={{0,7},{1,0},{2,1},{3,2},{4,3},{5,4},{6,5},{7,6},{8,15},{9,8},{10,9... | collective-permute-start | bytes 589832 | tf_op jit(solution)/shard_map/ppermute | solution.py:327
  96.8 11.1 %collective-permute-start.13 = (bf16[256,384]{1,0:T(8,128)(2,1)S(1)}, bf16[256,384]{1,0:T(8,128)(2,1)S(1)}, u32[]{:S(2)}, u32[]{:S(2)}) collective-permute-start(bf16[256,384]{1,0:T(8,128)(2,1)S(1)} %collective-permute-done.11.refs_8_), channel_id=1, source_target_pairs={{0,1},{1,2},{2,3},{3,4},{4,5},{5,6},{6,7},{7,0},{8,9},{9,10},{10,1... | collective-permute-start | bytes 589832 | tf_op jit(solution)/shard_map/ppermute | solution.py:327
  96.8 11.1 %collective-permute-start.14 = (bf16[256,384]{1,0:T(8,128)(2,1)S(1)}, bf16[256,384]{1,0:T(8,128)(2,1)S(1)}, u32[]{:S(2)}, u32[]{:S(2)}) collective-permute-start(bf16[256,384]{1,0:T(8,128)(2,1)S(1)} %collective-permute-done.12.refs_9_), channel_id=1, source_target_pairs={{0,7},{1,0},{2,1},{3,2},{4,3},{5,4},{6,5},{7,6},{8,15},{9,8},{10,9... | collective-permute-start | bytes 589832 | tf_op jit(solution)/shard_map/ppermute | solution.py:327
  104.5 8.7 %collective-permute-start.9 = (bf16[256,384]{1,0:T(8,128)(2,1)S(1)}, bf16[256,384]{1,0:T(8,128)(2,1)S(1)}, u32[]{:S(2)}, u32[]{:S(2)}) collective-permute-start(bf16[256,384]{1,0:T(8,128)(2,1)S(1)} %collective-permute-done.5.refs_6_), channel_id=1, source_target_pairs={{0,1},{1,2},{2,3},{3,4},{4,5},{5,6},{6,7},{7,0},{8,9},{9,10},{10,1... | collective-permute-start | bytes 589832 | tf_op jit(solution)/shard_map/ppermute | solution.py:327
  107.9 9.3 %collective-permute-start.16 = (bf16[256,384]{1,0:T(8,128)(2,1)S(1)}, bf16[256,384]{1,0:T(8,128)(2,1)S(1)}, u32[]{:S(2)}, u32[]{:S(2)}) collective-permute-start(bf16[256,384]{1,0:T(8,128)(2,1)S(1)} %collective-permute-done.14.refs_9_), channel_id=1, source_target_pairs={{0,7},{1,0},{2,1},{3,2},{4,3},{5,4},{6,5},{7,6},{8,15},{9,8},{10,9... | collective-permute-start | bytes 589832 | tf_op jit(solution)/shard_map/ppermute | solution.py:327
  113.3 9.3 %collective-permute-start.15 = (bf16[256,384]{1,0:T(8,128)(2,1)S(1)}, bf16[256,384]{1,0:T(8,128)(2,1)S(1)}, u32[]{:S(2)}, u32[]{:S(2)}) collective-permute-start(bf16[256,384]{1,0:T(8,128)(2,1)S(1)} %collective-permute-done.9.refs_0_), channel_id=1, source_target_pairs={{0,1},{1,2},{2,3},{3,4},{4,5},{5,6},{6,7},{7,0},{8,9},{9,10},{10,1... | collective-permute-start | bytes 589832 | tf_op jit(solution)/shard_map/ppermute | solution.py:327
  119.3 10.7 %collective-permute-start.24 = (bf16[256,384]{1,0:T(8,128)(2,1)S(1)}, bf16[256,384]{1,0:T(8,128)(2,1)S(1)}, u32[]{:S(2)}, u32[]{:S(2)}) collective-permute-start(bf16[256,384]{1,0:T(8,128)(2,1)S(1)} %get-tuple-element.215), channel_id=1, source_target_pairs={{0,1},{1,2},{2,3},{3,4},{4,5},{5,6},{6,7},{7,0},{8,9},{9,10},{10,1... | collective-permute-start | bytes 589832 | tf_op jit(solution)/shard_map/ppermute | solution.py:327
  119.3 10.6 %collective-permute-start.25 = (bf16[256,384]{1,0:T(8,128)(2,1)S(1)}, bf16[256,384]{1,0:T(8,128)(2,1)S(1)}, u32[]{:S(2)}, u32[]{:S(2)}) collective-permute-start(bf16[256,384]{1,0:T(8,128)(2,1)S(1)} %get-tuple-element.216), channel_id=1, source_target_pairs={{0,7},{1,0},{2,1},{3,2},{4,3},{5,4},{6,5},{7,6},{8,15},{9,8},{10,9... | collective-permute-start | bytes 589832 | tf_op jit(solution)/shard_map/ppermute | solution.py:327
  124.6 8.9 %collective-permute-start.17 = (bf16[256,384]{1,0:T(8,128)(2,1)S(1)}, bf16[256,384]{1,0:T(8,128)(2,1)S(1)}, u32[]{:S(2)}, u32[]{:S(2)}) collective-permute-start(bf16[256,384]{1,0:T(8,128)(2,1)S(1)} %get-tuple-element.201), channel_id=1, source_target_pairs={{0,1},{1,2},{2,3},{3,4},{4,5},{5,6},{6,7},{7,0},{8,9},{9,10},{10,1... | collective-permute-start | bytes 589832 | tf_op jit(solution)/shard_map/ppermute | solution.py:327
  133.5 8.9 %collective-permute-start.19 = (bf16[256,384]{1,0:T(8,128)(2,1)S(1)}, bf16[256,384]{1,0:T(8,128)(2,1)S(1)}, u32[]{:S(2)}, u32[]{:S(2)}) collective-permute-start(bf16[256,384]{1,0:T(8,128)(2,1)S(1)} %add_convert_fusion.11), channel_id=1, source_target_pairs={{0,1},{1,2},{2,3},{3,4},{4,5},{5,6},{6,7},{7,0},{8,9},{9,10},{10,1... | collective-permute-start | bytes 589832 | tf_op jit(solution)/shard_map/ppermute | solution.py:327
  133.7 9.0 %collective-permute-start.20 = (bf16[256,384]{1,0:T(8,128)(2,1)S(1)}, bf16[256,384]{1,0:T(8,128)(2,1)S(1)}, u32[]{:S(2)}, u32[]{:S(2)}) collective-permute-start(bf16[256,384]{1,0:T(8,128)(2,1)S(1)} %add_convert_fusion.10), channel_id=1, source_target_pairs={{0,7},{1,0},{2,1},{3,2},{4,3},{5,4},{6,5},{7,6},{8,15},{9,8},{10,9... | collective-permute-start | bytes 589832 | tf_op jit(solution)/shard_map/ppermute | solution.py:327
  138.7 9.4 %collective-permute-start.28 = (bf16[256,384]{1,0:T(8,128)(2,1)S(1)}, bf16[256,384]{1,0:T(8,128)(2,1)S(1)}, u32[]{:S(2)}, u32[]{:S(2)}) collective-permute-start(bf16[256,384]{1,0:T(8,128)(2,1)S(1)} %add_convert_fusion.3), channel_id=1, source_target_pairs={{0,1},{1,2},{2,3},{3,4},{4,5},{5,6},{6,7},{7,0},{8,9},{9,10},{10,1... | collective-permute-start | bytes 589832 | tf_op jit(solution)/shard_map/ppermute | solution.py:327
  138.8 9.2 %collective-permute-start.29 = (bf16[256,384]{1,0:T(8,128)(2,1)S(1)}, bf16[256,384]{1,0:T(8,128)(2,1)S(1)}, u32[]{:S(2)}, u32[]{:S(2)}) collective-permute-start(bf16[256,384]{1,0:T(8,128)(2,1)S(1)} %add_convert_fusion.2), channel_id=1, source_target_pairs={{0,7},{1,0},{2,1},{3,2},{4,3},{5,4},{6,5},{7,6},{8,15},{9,8},{10,9... | collective-permute-start | bytes 589832 | tf_op jit(solution)/shard_map/ppermute | solution.py:327
  (11 other events, 74.1 us)
